TPU v7x, 256 devices: a whole 4x4x8 slice. The times are simulated.
256 devices in a mesh: frame: 32 (over z_lo, x, core), row: 8 (over y, z_hi).
Axes of the slice: x: 4, y: 4, z: 8 (z_hi: 2, z_lo: 4; z = z_hi * 4 + z_lo), core: 2. Of those that a mesh axis runs over, the one named last changes fastest.
Arguments:
- frames: bfloat16 [32, 32, 384, 128], P('frame', 'row'), may hold values from -20 to 20
- norm_gain: float32 [128], replicated, may hold values from 0.5 to 1.5
- qkv_weight: bfloat16 [3, 128, 128], replicated, may hold values from -12 to 12
- out_weight: bfloat16 [128, 128], replicated, may hold values from -0.5 to 0.5
- conv_weight: bfloat16 [3, 3, 128, 128], replicated, may hold values from -0.1875 to 0.1875
- out_grad: bfloat16 [32, 32, 384, 128], P('frame', 'row'), may hold values from -6 to 6
Outputs:
- output: bfloat16 [32, 32, 384, 128], P('frame', 'row')
- grad_frames: bfloat16 [32, 32, 384, 128], P('frame', 'row')
- grad_gain: float32 [128], replicated
- grad_qkv: float32 [3, 128, 128], replicated
- grad_out: float32 [128, 128], replicated
- grad_conv: float32 [3, 3, 128, 128], replicated
All inputs are finite; a program needn't handle non-finite values.
Results may differ from a plain program's by a relative error of at most 0.013.
The roundings to bfloat16 on the way count: a program that leaves them out, or rounds other values in their place, can miss the bound.
Values may be sent and summed in bfloat16 or wider, within the bound.
A program may use at most 64 MiB of HBM per device.

v0:
```python
import math

import jax
import jax.numpy as jnp
from jax import lax
from jax.sharding import PartitionSpec as P

HEADS = 4


EPSILON = 1e-05


def with_halo(array, sides, width):
    for axis, dim in sides:
        size, length = (lax.axis_size(axis), array.shape[dim])
        up = [(i, (i + 1) % size) for i in range(size - 1)]
        down = [(j, i) for i, j in up]
        last = lax.slice_in_dim(array, length - width, length, axis=dim)
        leading = lax.slice_in_dim(array, 0, width, axis=dim)
        before = lax.ppermute(last, axis, up)
        after = lax.ppermute(leading, axis, down)
        array = jnp.concatenate([before, array, after], axis=dim)
    return array


def normalize(frames, norm_gain):
    values = frames.astype(jnp.float32)
    center = jnp.mean(values, axis=-1, keepdims=True)
    spread = jnp.mean(jnp.square(values - center), axis=-1, keepdims=True)
    inverse = lax.rsqrt(spread + EPSILON)
    unit = (values - center) * inverse
    return (unit, inverse, (unit * norm_gain).astype(jnp.bfloat16))


def norm_back(grad_normed, unit, inverse, norm_gain):
    gscaled = grad_normed.astype(jnp.float32) * norm_gain
    first = jnp.mean(gscaled, axis=-1, keepdims=True)
    second = jnp.mean(gscaled * unit, axis=-1, keepdims=True)
    return inverse * (gscaled - first - unit * second)


def project(source, qkv_weight):
    flat = source.reshape(-1, source.shape[-1])
    return tuple(
        (
            jnp.dot(flat, qkv_weight[index], preferred_element_type=jnp.float32)
            .astype(jnp.bfloat16)
            .reshape(source.shape)
            for index in range(3)
        )
    )


def project_back(source, grads, qkv_weight):
    flat = source.reshape(-1, source.shape[-1])
    total = jnp.zeros(flat.shape, jnp.float32)
    wgrads = []
    for index in range(3):
        grad_flat = grads[index].reshape(flat.shape)
        total = total + jnp.dot(grad_flat, qkv_weight[index].T, preferred_element_type=jnp.float32)
        wgrads.append(
            lax.dot_general(
                flat, grad_flat, (((0,), (0,)), ((), ())), preferred_element_type=jnp.float32
            )
        )
    return (total.astype(jnp.bfloat16).reshape(source.shape), jnp.stack(wgrads))


def split_heads(values, heads):
    count, pixels, chans = values.shape
    return values.reshape(count, pixels, heads, chans // heads)


def attend(queries, keys_all, values_all, heads):
    count, pixels, chans = queries.shape
    factor = (chans // heads) ** (-0.5)
    scores = (
        jnp.einsum(
            "fnhd,gnhd->nhfg",
            split_heads(queries, heads),
            split_heads(keys_all, heads),
            preferred_element_type=jnp.float32,
        )
        * factor
    )
    probs = jax.nn.softmax(scores, axis=-1)
    weights = probs.astype(jnp.bfloat16)
    mixed = jnp.einsum(
        "nhfg,gnhd->fnhd",
        weights,
        split_heads(values_all, heads),
        preferred_element_type=jnp.float32,
    )
    return (probs, mixed.reshape(count, pixels, chans).astype(jnp.bfloat16))


def attend_back(probs, queries, keys_all, values_all, grad_mixed, heads):
    count, pixels, chans = queries.shape
    factor = (chans // heads) ** (-0.5)
    weights = probs.astype(jnp.bfloat16)
    grad_heads = split_heads(grad_mixed, heads)
    grad_values = jnp.einsum(
        "nhfg,fnhd->gnhd", weights, grad_heads, preferred_element_type=jnp.float32
    ).astype(jnp.bfloat16)
    grad_probs = jnp.einsum(
        "fnhd,gnhd->nhfg",
        grad_heads,
        split_heads(values_all, heads),
        preferred_element_type=jnp.float32,
    )
    grad_scores = probs * (grad_probs - jnp.sum(probs * grad_probs, axis=-1, keepdims=True))
    grad_scores = (grad_scores * factor).astype(jnp.bfloat16)
    grad_queries = jnp.einsum(
        "nhfg,gnhd->fnhd",
        grad_scores,
        split_heads(keys_all, heads),
        preferred_element_type=jnp.float32,
    ).astype(jnp.bfloat16)
    grad_keys = jnp.einsum(
        "nhfg,fnhd->gnhd",
        grad_scores,
        split_heads(queries, heads),
        preferred_element_type=jnp.float32,
    ).astype(jnp.bfloat16)
    shape = (count, pixels, chans)
    return (grad_queries.reshape(shape), grad_keys.reshape(shape), grad_values.reshape(shape))


def widen(padded):
    return jnp.pad(padded, ((0, 0), (0, 0), (1, 1), (0, 0)))


def convolve(padded, weight):
    full = widen(padded)
    count, tall, wide, chans = full.shape
    rows, width = (tall - 2, wide - 2)
    total = jnp.zeros((count * rows * width, chans), jnp.float32)
    for row_off in range(3):
        for col_off in range(3):
            slab = full[:, row_off : row_off + rows, col_off : col_off + width].reshape(-1, chans)
            total = total + jnp.dot(
                slab, weight[row_off, col_off], preferred_element_type=jnp.float32
            )
    return total.reshape(count, rows, width, chans)


def convolve_back(padded, weight):
    full = widen(padded)
    count, tall, wide, chans = full.shape
    rows, width = (tall - 2, wide - 2)
    total = jnp.zeros((count * rows * width, chans), jnp.float32)
    for row_off in range(3):
        for col_off in range(3):
            slab = full[
                :, 2 - row_off : 2 - row_off + rows, 2 - col_off : 2 - col_off + width
            ].reshape(-1, chans)
            total = total + jnp.dot(
                slab, weight[row_off, col_off].T, preferred_element_type=jnp.float32
            )
    return total.reshape(count, rows, width, chans)


def kernel_grad(padded, grads):
    full = widen(padded)
    count, tall, wide, chans = full.shape
    rows, width = (tall - 2, wide - 2)
    grad_flat = grads.reshape(-1, chans)
    result = []
    for row_off in range(3):
        for col_off in range(3):
            slab = full[:, row_off : row_off + rows, col_off : col_off + width].reshape(-1, chans)
            result.append(
                lax.dot_general(
                    slab, grad_flat, (((0,), (0,)), ((), ())), preferred_element_type=jnp.float32
                )
            )
    return jnp.stack(result).reshape(3, 3, chans, chans)


def on_device(frames, norm_gain, qkv_weight, out_weight, conv_weight, out_grad):
    count, rows, width, chans = frames.shape
    heads = HEADS
    pixels = rows * width
    unit, inverse, normed = normalize(frames, norm_gain)
    flat_normed = normed.reshape(count, pixels, chans)
    local_q, local_k, local_v = project(flat_normed, qkv_weight)
    queries, keys_all, values_all = (
        lax.all_to_all(local_q, "frame", split_axis=1, concat_axis=0, tiled=True),
        lax.all_to_all(local_k, "frame", split_axis=1, concat_axis=0, tiled=True),
        lax.all_to_all(local_v, "frame", split_axis=1, concat_axis=0, tiled=True),
    )
    probs, mixed_time = attend(queries, keys_all, values_all, heads)
    mixed = lax.all_to_all(mixed_time, "frame", split_axis=0, concat_axis=1, tiled=True)
    mixed_flat = mixed.reshape(-1, chans)
    hidden = frames.astype(jnp.float32) + jnp.dot(
        mixed_flat, out_weight, preferred_element_type=jnp.float32
    ).reshape(frames.shape)
    act = jax.nn.silu(hidden).astype(jnp.bfloat16)
    act_pad = with_halo(act, (("row", 1),), 1)
    output = (hidden + convolve(act_pad, conv_weight)).astype(jnp.bfloat16)
    grad_pad = with_halo(out_grad, (("row", 1),), 1)
    grad_act = convolve_back(grad_pad, conv_weight)
    sigma = jax.nn.sigmoid(hidden)
    grad_hidden = out_grad.astype(jnp.float32) + grad_act * sigma * (1.0 + hidden * (1.0 - sigma))
    grad_hidden_b = grad_hidden.astype(jnp.bfloat16).reshape(-1, chans)
    grad_out = lax.dot_general(
        mixed_flat, grad_hidden_b, (((0,), (0,)), ((), ())), preferred_element_type=jnp.float32
    )
    grad_mixed = (
        jnp.dot(grad_hidden_b, out_weight.T, preferred_element_type=jnp.float32)
        .astype(jnp.bfloat16)
        .reshape(count, pixels, chans)
    )
    grad_conv = kernel_grad(act_pad, out_grad)
    grad_mixed_time = lax.all_to_all(grad_mixed, "frame", split_axis=1, concat_axis=0, tiled=True)
    grad_q, grad_k, grad_v = attend_back(
        probs, queries, keys_all, values_all, grad_mixed_time, heads
    )
    back_q, back_k, back_v = (
        lax.all_to_all(grad_q, "frame", split_axis=0, concat_axis=1, tiled=True),
        lax.all_to_all(grad_k, "frame", split_axis=0, concat_axis=1, tiled=True),
        lax.all_to_all(grad_v, "frame", split_axis=0, concat_axis=1, tiled=True),
    )
    grad_normed, grad_qkv = project_back(flat_normed, (back_q, back_k, back_v), qkv_weight)
    grad_normed = grad_normed.reshape(frames.shape)
    grad_frames = (grad_hidden + norm_back(grad_normed, unit, inverse, norm_gain)).astype(
        jnp.bfloat16
    )
    grad_gain = jnp.sum((grad_normed.astype(jnp.float32) * unit).reshape(-1, chans), axis=0)
    summed = lax.psum((grad_gain, grad_qkv, grad_out, grad_conv), ("frame", "row"))
    total_pixels = count * lax.axis_size("frame") * rows * lax.axis_size("row") * width
    factor = 1.0 / math.sqrt(total_pixels)
    return (
        output,
        grad_frames,
        summed[0] * factor,
        summed[1] * factor,
        summed[2] * factor,
        summed[3] * factor,
    )


def solution(mesh):
    return jax.shard_map(
        on_device,
        mesh=mesh,
        in_specs=(P("frame", "row", None, None), P(), P(), P(), P(), P("frame", "row", None, None)),
        out_specs=(
            P("frame", "row", None, None),
            P("frame", "row", None, None),
            P(),
            P(),
            P(),
            P(),
        ),
        check_vma=False,
    )
```

profile of v0, /device:TPU:1, one launch (start us, length us, event | category | flops | bytes accessed | tf_op | source)
XLA Modules:
  0.0 671.6 jit_solution(15410568776958004409)
XLA Ops:
  8.2 9.6 %collective-permute-start.2 = (bf16[1,1,384,128]{3,2,1,0:T(8,128)(2,1)S(1)}, bf16[1,1,384,128]{3,2,1,0:T(8,128)(2,1)S(1)}, u32[]{:S(2)}, u32[]{:S(2)}) collective-permute-start(bf16[1,1,384,128]{3,2,1,0:T(8,128)(2,1)S(1)} %get-tuple-element.28), channel_id=1, source_target_pairs={{0,1},{1,2},{2,3},{3,4},{4,5},{5,6},{6,7},{8,9},{9,10},{10,11},{11... | collective-permute-start | bytes 294920 | tf_op jit(solution)/shard_map/ppermute | solution.py:21
  30.2 8.8 %reduce.15 = bf16[1536,128]{1,0:T(8,128)(2,1)S(1)} reduce(bf16[1536,1,128]{2,1,0:T(2,128)(2,1)S(1)} %bitcast.298, bf16[]{:T(256)} %broadcast.126), dimensions={1}, to_apply=%bitcast.277.reduce_sub_computation | reduce | bytes 786434
  39.9 7.1 %all-to-all-start.2 = ((bf16[32,2,3072]{2,1,0:T(2,128)(2,1)}), bf16[32,2,3072]{2,1,0:T(2,128)(2,1)S(1)}, u32[]{:S(2)}, u32[]{:S(2)}) async-start(bf16[32,2,3072]{2,1,0:T(2,128)(2,1)} %reshape.365), calls=%async_computation.2 | async-start | bytes 786432 | tf_op jit(solution)/shard_map/all_to_all | solution.py:190
  53.4 8.8 %reduce.14 = bf16[1536,128]{1,0:T(8,128)(2,1)S(1)} reduce(bf16[1536,1,128]{2,1,0:T(2,128)(2,1)S(1)} %bitcast.300, bf16[]{:T(256)} %broadcast.126), dimensions={1}, to_apply=%bitcast.278.reduce_sub_computation | reduce | bytes 786434
  69.4 8.8 %reduce.13 = bf16[1536,128]{1,0:T(8,128)(2,1)S(1)} reduce(bf16[1536,1,128]{2,1,0:T(2,128)(2,1)S(1)} %bitcast.301, bf16[]{:T(256)} %broadcast.126), dimensions={1}, to_apply=%bitcast.279.reduce_sub_computation | reduce | bytes 786434
  81.3 7.7 %all-to-all-start.1 = ((bf16[32,2,3072]{2,1,0:T(2,128)(2,1)}), bf16[32,2,3072]{2,1,0:T(2,128)(2,1)S(1)}, u32[]{:S(2)}, u32[]{:S(2)}) async-start(bf16[32,2,3072]{2,1,0:T(2,128)(2,1)} %reshape.363), calls=%async_computation.1 | async-start | bytes 786432 | tf_op jit(solution)/shard_map/all_to_all | solution.py:189
  92.2 10.6 %all-to-all-done.1 = bf16[32,2,3072]{2,1,0:T(2,128)(2,1)S(1)} async-done(((bf16[32,2,3072]{2,1,0:T(2,128)(2,1)}), bf16[32,2,3072]{2,1,0:T(2,128)(2,1)S(1)}, u32[]{:S(2)}, u32[]{:S(2)}) %all-to-all-start.1) | async-done | bytes 393248 | tf_op jit(solution)/shard_map/all_to_all | solution.py:189
  102.8 12.9 %all-to-all-start = ((bf16[32,2,3072]{2,1,0:T(2,128)(2,1)}), bf16[32,2,3072]{2,1,0:T(2,128)(2,1)}, u32[]{:S(2)}, u32[]{:S(2)}) async-start(bf16[32,2,3072]{2,1,0:T(2,128)(2,1)} %reshape.361), calls=%async_computation | async-start | bytes 786432 | tf_op jit(solution)/shard_map/all_to_all | solution.py:191
  119.3 6.6 bitcast_reduce_fusion.1
  125.9 7.3 %bitcast_reduce_fusion.2 = bf16[1536,128]{1,0:T(8,128)(2,1)} fusion(bf16[1536,1,128]{2,1,0:T(2,128)(2,1)S(1)} %reshape.364), kind=kLoop, calls=%fused_computation.208 | loop fusion | bytes 786432 | tf_op jit(solution)/shard_map/all_to_all | solution.py:189
  135.9 6.8 %bitcast_reduce_fusion.3 = bf16[1536,128]{1,0:T(8,128)(2,1)S(1)} fusion(bf16[1536,1,128]{2,1,0:T(2,128)(2,1)S(1)} %reshape.362), kind=kLoop, calls=%fused_computation.209 | loop fusion | bytes 786432 | tf_op jit(solution)/shard_map/all_to_all | solution.py:191
  165.2 7.6 %all-to-all-start.3 = ((bf16[32,48,128]{2,1,0:T(8,128)(2,1)}), bf16[32,48,128]{2,1,0:T(8,128)(2,1)}, u32[]{:S(2)}, u32[]{:S(2)}) async-start(bf16[32,48,128]{2,1,0:T(8,128)(2,1)} %copy.73), calls=%async_computation.3 | async-start | bytes 786432 | tf_op jit(solution)/shard_map/all_to_all | solution.py:194
  177.2 9.5 %all-to-all-done.3 = bf16[32,48,128]{2,1,0:T(8,128)(2,1)} async-done(((bf16[32,48,128]{2,1,0:T(8,128)(2,1)}), bf16[32,48,128]{2,1,0:T(8,128)(2,1)}, u32[]{:S(2)}, u32[]{:S(2)}) %all-to-all-start.3) | async-done | bytes 393248 | tf_op jit(solution)/shard_map/all_to_all | solution.py:194
  188.2 8.2 %collective-permute-start = (bf16[1,1,384,128]{3,2,1,0:T(8,128)(2,1)S(1)}, bf16[1,1,384,128]{3,2,1,0:T(8,128)(2,1)S(1)}, u32[]{:S(2)}, u32[]{:S(2)}) collective-permute-start(bf16[1,1,384,128]{3,2,1,0:T(8,128)(2,1)S(1)} %get-tuple-element.32), channel_id=1, source_target_pairs={{0,1},{1,2},{2,3},{3,4},{4,5},{5,6},{6,7},{8,9},{9,10},{10,11},{11... | collective-permute-start | bytes 294920 | tf_op jit(solution)/shard_map/ppermute | solution.py:21
  213.7 6.5 copy.125
  220.2 8.8 %reduce.16 = bf16[1536,128]{1,0:T(8,128)(2,1)S(1)} reduce(bf16[1536,1,128]{2,1,0:T(2,128)(2,1)S(1)} %bitcast.299, bf16[]{:T(256)} %broadcast.126), dimensions={1}, to_apply=%bitcast.276.reduce_sub_computation | reduce | bytes 786434
  229.9 7.9 %all-to-all-start.4 = ((bf16[32,2,3072]{2,1,0:T(2,128)(2,1)}), bf16[32,2,3072]{2,1,0:T(2,128)(2,1)S(1)}, u32[]{:S(2)}, u32[]{:S(2)}) async-start(bf16[32,2,3072]{2,1,0:T(2,128)(2,1)} %reshape.367), calls=%async_computation.4 | async-start | bytes 786432 | tf_op jit(solution)/shard_map/all_to_all | solution.py:216
  241.5 9.9 %all-to-all-done.4 = bf16[32,2,3072]{2,1,0:T(2,128)(2,1)S(1)} async-done(((bf16[32,2,3072]{2,1,0:T(2,128)(2,1)}), bf16[32,2,3072]{2,1,0:T(2,128)(2,1)S(1)}, u32[]{:S(2)}, u32[]{:S(2)}) %all-to-all-start.4) | async-done | bytes 393248 | tf_op jit(solution)/shard_map/all_to_all | solution.py:216
  251.8 6.6 bitcast_reduce_fusion
  267.6 7.5 %fusion.22 = bf16[48,4,32,32]{3,2,1,0:T(8,128)(2,1)} fusion(bf16[32,48,4,32]{0,3,2,1:T(8,128)(2,1)} %copy.78, f32[48,4,32,32]{2,3,1,0:T(8,128)} %fusion.32, f32[48,4,32,32]{2,3,1,0:T(8,128)} %get-tuple-element.35, f32[48,4,32]{2,1,0:T(4,128)} %copy-done.18), kind=kOutput, calls=%fused_computation.40 | convolution fusion | flops 14161951 | bytes 2383872 | tf_op jit(solution)/shard_map/nhfg,gnhd->fnhd/dot_general | solution.py:114
  301.7 7.6 %fusion.25 = bf16[48,4,32,32]{3,2,1,0:T(8,128)(2,1)} fusion(bf16[32,48,4,32]{0,3,2,1:T(8,128)(2,1)} %copy.81, f32[48,4,32,32]{2,3,1,0:T(8,128)} %fusion.32, f32[48,4,32,32]{2,3,1,0:T(8,128)} %get-tuple-element.35, f32[48,4,32]{2,1,0:T(4,128)S(1)} %copy-done.19), kind=kOutput, calls=%fused_computation.41 | convolution fusion | flops 14161951 | bytes 2383872 | tf_op jit(solution)/shard_map/nhfg,fnhd->gnhd/dot_general | solution.py:120
  324.4 8.9 %all-to-all-done.6 = bf16[32,48,128]{2,1,0:T(8,128)(2,1)S(1)} async-done(((bf16[32,48,128]{2,1,0:T(8,128)(2,1)}), bf16[32,48,128]{2,1,0:T(8,128)(2,1)S(1)}, u32[]{:S(2)}, u32[]{:S(2)}) %all-to-all-start.6) | async-done | bytes 393248 | tf_op jit(solution)/shard_map/all_to_all | solution.py:222
  335.1 74.6 %psum.28 = f32[128]{0:T(128)S(1)} all-reduce(f32[128]{0:T(128)S(1)} %get-tuple-element.6), channel_id=1, replica_groups=mesh['frame'=32,'row'=8] {'frame','row'}, use_global_device_ids=true, to_apply=%region_8.9 | all-reduce | flops 128 | bytes 1024 | tf_op jit(solution)/shard_map/psum | solution.py:231
  412.6 246.9 %all-reduce.5.cloned.1.call-done = (f32[3,128,128]{2,1,0:T(8,128)}, f32[128,128]{1,0:T(8,128)}, f32[3,3,128,128]{3,2,1,0:T(8,128)}) async-done(((f32[3,128,128]{2,1,0:T(8,128)}, f32[128,128]{1,0:T(8,128)}, f32[3,3,128,128]{3,2,1,0:T(8,128)}), (f32[3,128,128]{2,1,0:T(8,128)}, f32[128,128]{1,0:T(8,128)}, f32[3,3,128,128]{3,2,1,0:T(8,128)})) %all-reduce.5.cloned.1.call-update) | async-done | bytes 851984 | tf_op jit(solution)/shard_map/psum | solution.py:231
  (145 shorter events, 150.9 us)
Async XLA Ops:
  7.2 179.5 %copy-start = (bf16[128,128]{1,0:T(8,128)(2,1)S(1)}, bf16[128,128]{1,0:T(8,128)(2,1)}, u32[]{:S(2)}) copy-start(bf16[128,128]{1,0:T(8,128)(2,1)} %param.9) | copy-start | bytes 98308
  7.2 16.1 %copy-start.16 = (bf16[3,128,128]{2,1,0:T(8,128)(2,1)S(1)}, bf16[3,128,128]{2,1,0:T(8,128)(2,1)}, u32[]{:S(2)}) copy-start(bf16[3,128,128]{2,1,0:T(8,128)(2,1)} %param.8) | copy-start | bytes 294916
  8.2 70.9 %collective-permute-start.2 = (bf16[1,1,384,128]{3,2,1,0:T(8,128)(2,1)S(1)}, bf16[1,1,384,128]{3,2,1,0:T(8,128)(2,1)S(1)}, u32[]{:S(2)}, u32[]{:S(2)}) collective-permute-start(bf16[1,1,384,128]{3,2,1,0:T(8,128)(2,1)S(1)} %get-tuple-element.28), channel_id=1, source_target_pairs={{0,1},{1,2},{2,3},{3,4},{4,5},{5,6},{6,7},{8,9},{9,10},{10,11},{11... | collective-permute-start | bytes 294920 | tf_op jit(solution)/shard_map/ppermute | solution.py:21
  17.8 61.2 %collective-permute-start.3 = (bf16[1,1,384,128]{3,2,1,0:T(8,128)(2,1)S(1)}, bf16[1,1,384,128]{3,2,1,0:T(8,128)(2,1)S(1)}, u32[]{:S(2)}, u32[]{:S(2)}) collective-permute-start(bf16[1,1,384,128]{3,2,1,0:T(8,128)(2,1)S(1)} %get-tuple-element.29), channel_id=1, source_target_pairs={{1,0},{2,1},{3,2},{4,3},{5,4},{6,5},{7,6},{9,8},{10,9},{11,10},{12... | collective-permute-start | bytes 294920 | tf_op jit(solution)/shard_map/ppermute | solution.py:22
  39.9 41.4 %all-to-all-start.2 = ((bf16[32,2,3072]{2,1,0:T(2,128)(2,1)}), bf16[32,2,3072]{2,1,0:T(2,128)(2,1)S(1)}, u32[]{:S(2)}, u32[]{:S(2)}) async-start(bf16[32,2,3072]{2,1,0:T(2,128)(2,1)} %reshape.365), calls=%async_computation.2 | async-start | bytes 786432 | tf_op jit(solution)/shard_map/all_to_all | solution.py:190
  63.3 15.8 %copy-start.2 = (bf16[1,4,384,128]{3,2,1,0:T(8,128)(2,1)S(1)}, bf16[1,4,384,128]{3,2,1,0:T(8,128)(2,1)}, u32[]{:S(2)}) copy-start(bf16[1,4,384,128]{3,2,1,0:T(8,128)(2,1)} %param.11) | copy-start | bytes 1179652
  81.3 21.5 %all-to-all-start.1 = ((bf16[32,2,3072]{2,1,0:T(2,128)(2,1)}), bf16[32,2,3072]{2,1,0:T(2,128)(2,1)S(1)}, u32[]{:S(2)}, u32[]{:S(2)}) async-start(bf16[32,2,3072]{2,1,0:T(2,128)(2,1)} %reshape.363), calls=%async_computation.1 | async-start | bytes 786432 | tf_op jit(solution)/shard_map/all_to_all | solution.py:189
  102.8 30.4 %all-to-all-start = ((bf16[32,2,3072]{2,1,0:T(2,128)(2,1)}), bf16[32,2,3072]{2,1,0:T(2,128)(2,1)}, u32[]{:S(2)}, u32[]{:S(2)}) async-start(bf16[32,2,3072]{2,1,0:T(2,128)(2,1)} %reshape.361), calls=%async_computation | async-start | bytes 786432 | tf_op jit(solution)/shard_map/all_to_all | solution.py:191
  162.8 11.1 %copy-start.9 = (f32[1536,128]{1,0:T(8,128)S(1)}, f32[1536,128]{1,0:T(8,128)}, u32[]{:S(2)}) copy-start(f32[1536,128]{1,0:T(8,128)} %convolution_add_fusion.5) | copy-start | bytes 2359300
  165.2 21.4 %all-to-all-start.3 = ((bf16[32,48,128]{2,1,0:T(8,128)(2,1)}), bf16[32,48,128]{2,1,0:T(8,128)(2,1)}, u32[]{:S(2)}, u32[]{:S(2)}) async-start(bf16[32,48,128]{2,1,0:T(8,128)(2,1)} %copy.73), calls=%async_computation.3 | async-start | bytes 786432 | tf_op jit(solution)/shard_map/all_to_all | solution.py:194
  173.9 12.8 %copy-start.3 = (bf16[1,4,384,128]{3,2,1,0:T(8,128)(2,1)S(1)}, bf16[1,4,384,128]{3,2,1,0:T(8,128)(2,1)}, u32[]{:S(2)}) copy-start(bf16[1,4,384,128]{3,2,1,0:T(8,128)(2,1)} %param.6) | copy-start | bytes 1179652
  186.7 11.1 %copy-start.14 = (bf16[1,4,384,128]{3,2,1,0:T(8,128)(2,1)S(1)}, bf16[1,4,384,128]{3,2,1,0:T(8,128)(2,1)}, u32[]{:S(2)}) copy-start(bf16[1,4,384,128]{3,2,1,0:T(8,128)(2,1)} %get-tuple-element.26) | copy-start | bytes 1179652
  186.7 11.1 %copy-start.15 = (bf16[3,3,128,128]{3,2,1,0:T(8,128)(2,1)S(1)}, bf16[3,3,128,128]{3,2,1,0:T(8,128)(2,1)}, u32[]{:S(2)}) copy-start(bf16[3,3,128,128]{3,2,1,0:T(8,128)(2,1)} %param.10) | copy-start | bytes 884740
  188.2 12.0 %collective-permute-start = (bf16[1,1,384,128]{3,2,1,0:T(8,128)(2,1)S(1)}, bf16[1,1,384,128]{3,2,1,0:T(8,128)(2,1)S(1)}, u32[]{:S(2)}, u32[]{:S(2)}) collective-permute-start(bf16[1,1,384,128]{3,2,1,0:T(8,128)(2,1)S(1)} %get-tuple-element.32), channel_id=1, source_target_pairs={{0,1},{1,2},{2,3},{3,4},{4,5},{5,6},{6,7},{8,9},{9,10},{10,11},{11... | collective-permute-start | bytes 294920 | tf_op jit(solution)/shard_map/ppermute | solution.py:21
  196.4 10.0 %collective-permute-start.1 = (bf16[1,1,384,128]{3,2,1,0:T(8,128)(2,1)S(1)}, bf16[1,1,384,128]{3,2,1,0:T(8,128)(2,1)S(1)}, u32[]{:S(2)}, u32[]{:S(2)}) collective-permute-start(bf16[1,1,384,128]{3,2,1,0:T(8,128)(2,1)S(1)} %get-tuple-element.33), channel_id=1, source_target_pairs={{1,0},{2,1},{3,2},{4,3},{5,4},{6,5},{7,6},{9,8},{10,9},{11,10},{12... | collective-permute-start | bytes 294920 | tf_op jit(solution)/shard_map/ppermute | solution.py:22
  229.9 21.6 %all-to-all-start.4 = ((bf16[32,2,3072]{2,1,0:T(2,128)(2,1)}), bf16[32,2,3072]{2,1,0:T(2,128)(2,1)S(1)}, u32[]{:S(2)}, u32[]{:S(2)}) async-start(bf16[32,2,3072]{2,1,0:T(2,128)(2,1)} %reshape.367), calls=%async_computation.4 | async-start | bytes 786432 | tf_op jit(solution)/shard_map/all_to_all | solution.py:216
  277.5 18.1 %all-to-all-start.5 = ((bf16[32,48,128]{2,1,0:T(8,128)(2,1)}), bf16[32,48,128]{2,1,0:T(8,128)(2,1)}, u32[]{:S(2)}, u32[]{:S(2)}) async-start(bf16[32,48,128]{2,1,0:T(8,128)(2,1)} %copy.80), calls=%async_computation.5 | async-start | bytes 786432 | tf_op jit(solution)/shard_map/all_to_all | solution.py:221
  286.9 12.9 %copy-start.8 = (bf16[1,4,384,128]{3,2,1,0:T(8,128)(2,1)S(1)}, bf16[1,4,384,128]{3,2,1,0:T(8,128)(2,1)}, u32[]{:S(2)}) copy-start(bf16[1,4,384,128]{3,2,1,0:T(8,128)(2,1)} %copy-done.7) | copy-start | bytes 1179652
  289.3 12.4 %copy-start.19 = (f32[48,4,32]{2,1,0:T(4,128)S(1)}, f32[48,4,32]{2,1,0:T(4,128)}, u32[]{:S(2)}) copy-start(f32[48,4,32]{2,1,0:T(4,128)} %copy-done.18) | copy-start | bytes 73732
  295.6 17.9 %all-to-all-start.7 = ((bf16[32,48,128]{2,1,0:T(8,128)(2,1)}), bf16[32,48,128]{2,1,0:T(8,128)(2,1)S(1)}, u32[]{:S(2)}, u32[]{:S(2)}) async-start(bf16[32,48,128]{2,1,0:T(8,128)(2,1)} %copy.86), calls=%async_computation.7 | async-start | bytes 786432 | tf_op jit(solution)/shard_map/all_to_all | solution.py:223
  313.5 19.8 %all-to-all-start.6 = ((bf16[32,48,128]{2,1,0:T(8,128)(2,1)}), bf16[32,48,128]{2,1,0:T(8,128)(2,1)S(1)}, u32[]{:S(2)}, u32[]{:S(2)}) async-start(bf16[32,48,128]{2,1,0:T(8,128)(2,1)} %copy.83), calls=%async_computation.6 | async-start | bytes 786432 | tf_op jit(solution)/shard_map/all_to_all | solution.py:222
  319.5 340.0 %all-reduce.5.cloned.1.call-start = ((), (), s32[]{:S(2)}) async-start(), calls=%async_computation.8 | async-start | bytes 1703936 | tf_op jit(solution)/shard_map/psum | solution.py:231
  334.3 76.6 %copy-start.11 = (f32[1,4,384,128]{3,2,1,0:T(8,128)S(1)}, f32[1,4,384,128]{3,2,1,0:T(8,128)}, u32[]{:S(2)}) copy-start(f32[1,4,384,128]{3,2,1,0:T(8,128)} %get-tuple-element.12) | copy-start | bytes 2359300
  410.9 253.6 %copy-start.1 = (bf16[128,128]{1,0:T(8,128)(2,1)S(1)}, bf16[128,128]{1,0:T(8,128)(2,1)}, u32[]{:S(2)}) copy-start(bf16[128,128]{1,0:T(8,128)(2,1)} %param.9) | copy-start | bytes 98308
  (9 other events, 48.0 us)
Sparse Core Ops, SparseCore 0:
  410.5 248.9 all-reduce.4
where the time goes:
time: 676 us; the launch traced here: 672 us
  waiting for transfers between devices  302 us (45%)
  local copies, waits for them, and re-layouts  88.4 us (13%)
  starting transfers between devices  78.3 us (12%)
  blocking collectives  74.6 us (11%)
  matrix products  62.5 us (9%)
  other arithmetic  50.6 us (7%)
  between operations  14.9 us (2%)
    psum x1, waiting for transfers between devices, on_device(): lax.psum((grad_gain, grad_qkv, grad_out, grad_conv), ('frame', 'row'))  247 us
    psum x1, blocking collectives, on_device(): lax.psum((grad_gain, grad_qkv, grad_out, grad_conv), ('frame', 'row'))  74.6 us
    unnamed x4, other arithmetic  35.2 us
    reshape x3, local copies, waits for them, and re-layouts, project(): return tuple((jnp.dot(flat, qkv_weight[index], preferred_element_type=jnp...  18.4 us
    ppermute x2, starting transfers between devices, with_halo(): before = lax.ppermute(last, axis, up)  17.9 us
    reshape x7, local copies, waits for them, and re-layouts, split_heads(): return values.reshape(count, pixels, heads, chans // heads)  15.5 us
  transfers between devices with their start and end apart: 13, of which 9 were waited for; matrix products, arithmetic and copies ran while one was open for 16% of the time, Pallas kernels for 0%

commit v1 on v0

v1 whole, which is shorter than its diff:
```python
import math

import jax
import jax.numpy as jnp
from jax import lax
from jax.experimental import pallas as pl
from jax.experimental.pallas import tpu as pltpu
from jax.sharding import PartitionSpec as P

HEADS = 4
EPSILON = 1e-05
MESH = pl.DeviceIdType.MESH
F32 = jnp.float32
BF16 = jnp.bfloat16

NF = 32
NR = 8
C = 128
D = C // HEADS
ROWS = 4
W = 384
PIX = ROWS * W
NC = 3
CP = PIX // NC
M = CP // NF
NG = M // 8
G = 8 * NF

EP = 160
LP = 64
EB = EP // 16
LB = LP // 16


def nn(a, b):
    return jnp.dot(a, b, preferred_element_type=F32)


def nt(a, b):
    return lax.dot_general(a, b, (((1,), (1,)), ((), ())), preferred_element_type=F32)


def tn(a, b):
    return lax.dot_general(a, b, (((0,), (0,)), ((), ())), preferred_element_type=F32)


def rows_of(start, size):
    return pl.ds(pl.multiple_of(start, size), size)


def normalize(values):
    center = jnp.mean(values, axis=-1, keepdims=True)
    spread = jnp.mean(jnp.square(values - center), axis=-1, keepdims=True)
    inverse = lax.rsqrt(spread + EPSILON)
    return (values - center) * inverse, inverse


def kernel(
    factor,
    x_ref, gain_ref, wqkv_ref, wout_ref, wconv_ref, og_ref,
    out_ref, gf_ref, ggain_ref, gqkv_ref, gout_ref, gconv_ref,
    xt, unit_t, stage, k_t, v_s, q_s, n_s, probs,
    mix_s, mix_f, gm_s, gm_t, gn_s, gn_f,
    ogp, actp, gact, hid, gh, act_t, og_sh,
    acc_qkv, acc_gain, acc_out, acc_conv,
    e_s, e_r, e_b, e_br, e_g, e_f,
    l_s, l_r, l_b, l_br, l_g, l_f,
    snd, rcv, hsnd, hrcv, wsnd, wrcv,
):
    f = lax.axis_index("frame")
    r = lax.axis_index("row")
    core = lax.rem(f, 2)
    fx = f // 2
    y = r // 2
    zh = lax.rem(r, 2)
    a = y * 2 + core
    q = zh * 16 + fx

    def frame_peer(k):
        return lax.rem(f + k, NF)

    def a_peer(k):
        a2 = lax.rem(a + k, 8)
        return a2, (fx * 2 + lax.rem(a2, 2), (a2 // 2) * 2 + zh)

    def q_device(q2):
        return (lax.rem(q2, 16) * 2 + core, y * 2 + q2 // 16)

    barrier = pltpu.get_barrier_semaphore()

    @pl.loop(1, NF)
    def _(k):
        pl.semaphore_signal(barrier, inc=1, device_id=(frame_peer(k), r), device_id_type=MESH)
        pl.semaphore_signal(barrier, inc=1, device_id=q_device(lax.rem(q + k, 32)), device_id_type=MESH)

    @pl.loop(1, 8)
    def _(k):
        pl.semaphore_signal(barrier, inc=1, device_id=a_peer(k)[1], device_id_type=MESH)

    @pl.when(r > 0)
    def _():
        pl.semaphore_signal(barrier, inc=1, device_id=(f, r - 1), device_id_type=MESH)

    @pl.when(r < NR - 1)
    def _():
        pl.semaphore_signal(barrier, inc=1, device_id=(f, r + 1), device_id_type=MESH)

    pl.semaphore_wait(barrier, 31 + 31 + 7 + jnp.where(r > 0, 1, 0) + jnp.where(r < NR - 1, 1, 0))

    def to_time(phase, c, src, dst):
        @pl.loop(1, NF)
        def _(k):
            d = frame_peer(k)
            pltpu.make_async_remote_copy(
                src.at[rows_of(c * CP + d * M, M)], dst.at[rows_of(c * CP + f * M, M)],
                snd.at[phase, c], rcv.at[phase, c], device_id=(d, r), device_id_type=MESH,
            ).start()

        own = rows_of(c * CP + f * M, M)
        dst[own, :] = src[own, :]

    def arrived(phase, c, dst):
        view = dst.at[pl.ds(pl.multiple_of(c * CP, M), (NF - 1) * M)]
        pltpu.make_async_copy(view, view, rcv.at[phase, c]).wait()

    def left(phase, c, src):
        view = src.at[pl.ds(pl.multiple_of(c * CP, M), (NF - 1) * M)]
        pltpu.make_async_copy(view, view, snd.at[phase, c]).wait()

    @pl.loop(0, NC)
    def _(c):
        to_time(0, c, x_ref, xt)

    def halo_up(src, dst, s):
        return pltpu.make_async_remote_copy(
            src.at[pl.ds(W, W)], dst.at[pl.ds(5 * W, W)], hsnd.at[s], hrcv.at[s],
            device_id=(f, r - 1), device_id_type=MESH)

    def halo_down(src, dst, s):
        return pltpu.make_async_remote_copy(
            src.at[pl.ds(4 * W, W)], dst.at[pl.ds(0, W)], hsnd.at[s], hrcv.at[s],
            device_id=(f, r + 1), device_id_type=MESH)

    ogp[pl.ds(W, PIX), :] = og_ref[...]

    @pl.when(r > 0)
    def _():
        halo_up(ogp, ogp, 0).start()

    @pl.when(r < NR - 1)
    def _():
        halo_down(ogp, ogp, 1).start()

    edge = jnp.zeros((W, C), BF16)

    @pl.when(r == 0)
    def _():
        ogp[pl.ds(0, W), :] = edge
        actp[pl.ds(0, W), :] = edge

    @pl.when(r == NR - 1)
    def _():
        ogp[pl.ds(5 * W, W), :] = edge
        actp[pl.ds(5 * W, W), :] = edge

    def halo_wait(src, dst, s):
        @pl.when(r > 0)
        def _():
            halo_up(src, dst, s).wait_send()
            halo_down(src, dst, s + 1).wait_recv()

        @pl.when(r < NR - 1)
        def _():
            halo_down(src, dst, s + 1).wait_send()
            halo_up(src, dst, s).wait_recv()

    gain = gain_ref[...]
    wcat = jnp.concatenate([wqkv_ref[0], wqkv_ref[1], wqkv_ref[2]], axis=1)
    scale = D ** (-0.5)
    sub = lax.broadcasted_iota(jnp.int32, (8, G), 0)
    lane = lax.broadcasted_iota(jnp.int32, (8, G), 1)
    diag = (sub == lax.rem(lane, 8)).astype(F32)
    chan = lax.broadcasted_iota(jnp.int32, (1, C), 1) // D
    head_of = [(chan == h).astype(BF16) for h in range(HEADS)]

    acc_qkv[...] = jnp.zeros_like(acc_qkv)
    acc_gain[...] = jnp.zeros_like(acc_gain)
    acc_out[...] = jnp.zeros_like(acc_out)
    acc_conv[...] = jnp.zeros_like(acc_conv)

    @pl.loop(0, NC)
    def _(c):
        arrived(0, c, xt)
        chunk = rows_of(c * CP, CP)
        unit, _ = normalize(xt[chunk, :].astype(F32))
        unit_t[chunk, :] = unit
        stage[...] = (unit * gain).reshape(NF, M, C)

        @pl.loop(0, NG)
        def _(j):
            g = c * NG + j
            eight = pl.ds(pl.multiple_of(j * 8, 8), 8)
            normed = stage[:, eight, :].reshape(G, C).astype(BF16)
            n_s[g] = normed
            qkv = nn(normed, wcat).astype(BF16)
            queries, keys, values = qkv[:, :C], qkv[:, C : 2 * C], qkv[:, 2 * C :]
            q_s[g] = queries
            v_s[g] = values
            q_tr = jnp.transpose(queries)
            k_tr = jnp.transpose(keys)
            v_tr = jnp.transpose(values)
            k_t[g] = k_tr
            parts = []
            for h in range(HEADS):
                s = nn(keys * head_of[h], q_tr).reshape(NF, 8, G)
                top = jnp.max(s, axis=0)
                e = jnp.exp((s - top[None]) * scale)
                inv = diag / jnp.sum(e, axis=0)
                p = (e * inv[None]).reshape(G, G)
                probs[g * HEADS + h] = p
                parts.append(nn(v_tr[h * D : (h + 1) * D], p.astype(BF16)))
            mixed = jnp.transpose(jnp.concatenate(parts, axis=0))
            stage[:, eight, :] = mixed.reshape(NF, 8, C)

        mix_s[chunk, :] = stage[...].reshape(CP, C).astype(BF16)
        to_time(1, c, mix_s, mix_f)

    halo_wait(ogp, ogp, 0)
    col = lax.broadcasted_iota(jnp.int32, (W, C), 0)
    first_col = col == 0
    last_col = col == W - 1

    def after(z):
        return jnp.where(last_col, 0.0, pltpu.roll(z, W - 1, 0))

    def before(z):
        return jnp.where(first_col, 0.0, pltpu.roll(z, 1, 0))

    @pl.loop(0, ROWS)
    def _(row):
        total = jnp.zeros((W, 3 * C), F32)
        for i in range(3):
            total = total + nt(ogp[rows_of((row + 2 - i) * W, W), :], wconv_ref[i])
        here = rows_of(row * W, W)
        gact[here, :] = after(total[:, :C]) + total[:, C : 2 * C] + before(total[:, 2 * C :])
        own = og_ref[here, :].astype(F32)
        og_sh[here, :] = jnp.concatenate(
            [after(own).astype(BF16), og_ref[here, :], before(own).astype(BF16)], axis=1)

    @pl.loop(0, NC)
    def _(c):
        arrived(1, c, mix_f)
        chunk = rows_of(c * CP, CP)
        mixed = mix_f[chunk, :]
        hidden = x_ref[chunk, :].astype(F32) + nn(mixed, wout_ref[...])
        sigma = 1.0 / (1.0 + jnp.exp(-hidden))
        hid[chunk, :] = hidden
        actp[pl.ds(pl.multiple_of(W + c * CP, 128), CP), :] = (hidden * sigma).astype(BF16)
        ghidden = og_ref[chunk, :].astype(F32) + gact[chunk, :] * sigma * (1.0 + hidden * (1.0 - sigma))
        gh[chunk, :] = ghidden
        ghb = ghidden.astype(BF16)
        gm_s[chunk, :] = nt(ghb, wout_ref[...]).astype(BF16)
        to_time(2, c, gm_s, gm_t)
        acc_out[...] += tn(mixed, ghb)

    @pl.when(r > 0)
    def _():
        halo_up(actp, actp, 2).start()

    @pl.when(r < NR - 1)
    def _():
        halo_down(actp, actp, 3).start()

    def sum_a_send(s, size, src, dst):
        @pl.loop(1, 8)
        def _(k):
            a2, dev = a_peer(k)
            pltpu.make_async_remote_copy(
                src.at[rows_of(a2 * size, size)], dst.at[rows_of(a * size, size)],
                wsnd.at[s], wrcv.at[s], device_id=dev, device_id_type=MESH).start()

        own = rows_of(a * size, size)
        dst[own, :] = src[own, :]

    def sum_b_send(s, size, base, src, mid, dst):
        view = src.at[pl.ds(0, 7 * size)]
        pltpu.make_async_copy(view, view, wrcv.at[s - 1]).wait()
        total = src[pl.ds(0, size), :].astype(F32)
        for k in range(1, 8):
            total = total + src[pl.ds(k * size, size), :].astype(F32)
        mid[...] = total.astype(BF16)

        @pl.loop(0, size // 16)
        def _(o):
            owner = base + o

            @pl.when(owner != q)
            def _():
                pltpu.make_async_remote_copy(
                    mid.at[rows_of(o * 16, 16)], dst.at[rows_of(q * 16, 16)],
                    wsnd.at[s], wrcv.at[s], device_id=q_device(owner), device_id_type=MESH).start()

            @pl.when(owner == q)
            def _():
                dst[rows_of(q * 16, 16), :] = mid[rows_of(o * 16, 16), :]

    def owns(size, base):
        return jnp.logical_and(q >= base, q < base + size // 16)

    def sum_b_back(s, size, base, src, dst):
        @pl.when(owns(size, base))
        def _():
            view = src.at[pl.ds(0, 31 * 16)]
            pltpu.make_async_copy(view, view, wrcv.at[s - 1]).wait()
            total = jnp.sum(src[...].astype(F32).reshape(32, 16, C), axis=0) * factor
            mine = rows_of((q - base) * 16, 16)
            dst[mine, :] = total.astype(BF16)

            @pl.loop(1, 32)
            def _(k):
                pltpu.make_async_remote_copy(
                    dst.at[mine], dst.at[mine], wsnd.at[s], wrcv.at[s],
                    device_id=q_device(lax.rem(q + k, 32)), device_id_type=MESH).start()

    def sum_a_back(s, size, base, src, dst):
        nblock = size // 16

        @pl.when(owns(size, base))
        def _():
            view = src.at[pl.ds(0, (nblock - 1) * 16)]
            pltpu.make_async_copy(view, view, wrcv.at[s - 1]).wait()

        @pl.when(jnp.logical_not(owns(size, base)))
        def _():
            view = src.at[pl.ds(0, nblock * 16)]
            pltpu.make_async_copy(view, view, wrcv.at[s - 1]).wait()

        own = rows_of(a * size, size)

        @pl.loop(1, 8)
        def _(k):
            pltpu.make_async_remote_copy(
                src, dst.at[own], wsnd.at[s], wrcv.at[s], device_id=a_peer(k)[1], device_id_type=MESH).start()

        dst[own, :] = src[...]

    def sum_finish(s, size, base, src, mid, back, dst):
        view = dst.at[pl.ds(0, 7 * size)]
        pltpu.make_async_copy(view, view, wrcv.at[s + 3]).wait()
        sent = src.at[pl.ds(0, 7 * size)]
        pltpu.make_async_copy(sent, sent, wsnd.at[s]).wait()
        nblock = size // 16

        @pl.when(owns(size, base))
        def _():
            few = mid.at[pl.ds(0, (nblock - 1) * 16)]
            pltpu.make_async_copy(few, few, wsnd.at[s + 1]).wait()
            many = back.at[pl.ds(0, 31 * 16)]
            pltpu.make_async_copy(many, many, wsnd.at[s + 2]).wait()

        @pl.when(jnp.logical_not(owns(size, base)))
        def _():
            few = mid.at[pl.ds(0, nblock * 16)]
            pltpu.make_async_copy(few, few, wsnd.at[s + 1]).wait()

        pltpu.make_async_copy(view, view, wsnd.at[s + 3]).wait()

    def conv_grad():
        halo_wait(actp, actp, 2)

        @pl.loop(0, ROWS + 2)
        def _(row):
            act_t[row] = jnp.transpose(actp[rows_of(row * W, W), :])

        @pl.loop(0, ROWS)
        def _(row):
            shifted = og_sh[rows_of(row * W, W), :]
            for i in range(3):
                acc_conv[i] += nn(act_t[row + i], shifted)

        for i in range(3):
            for j in range(3):
                at = (3 * i + j) * C
                e_s[at : at + C, :] = acc_conv[i, :, j * C : (j + 1) * C].astype(BF16)
        e_s[9 * C : 10 * C, :] = acc_out[...].astype(BF16)
        sum_a_send(0, EP, e_s, e_r)

    def conv_out():
        @pl.loop(0, ROWS)
        def _(row):
            total = jnp.zeros((W, 3 * C), F32)
            for i in range(3):
                wide = jnp.concatenate([wconv_ref[i, j * C : (j + 1) * C, :] for j in range(3)], axis=1)
                total = total + nn(actp[rows_of((row + i) * W, W), :], wide)
            here = rows_of(row * W, W)
            conv = before(total[:, :C]) + total[:, C : 2 * C] + after(total[:, 2 * C :])
            out_ref[here, :] = (hid[here, :] + conv).astype(BF16)

    @pl.loop(0, NC)
    def _(c):
        arrived(2, c, gm_t)
        chunk = rows_of(c * CP, CP)
        stage[...] = gm_t[chunk, :].astype(F32).reshape(NF, M, C)

        @pl.loop(0, NG)
        def _(j):
            g = c * NG + j
            eight = pl.ds(pl.multiple_of(j * 8, 8), 8)
            gmixed = stage[:, eight, :].reshape(G, C).astype(BF16)
            gm_tr = jnp.transpose(gmixed)
            queries, values, k_tr = q_s[g], v_s[g], k_t[g]
            gk = jnp.zeros((G, C), F32)
            gv = jnp.zeros((G, C), F32)
            parts = []
            for h in range(HEADS):
                gp = nn(values * head_of[h], gm_tr).reshape(NF, 8, G)
                p = probs[g * HEADS + h]
                p3 = p.reshape(NF, 8, G)
                dot = jnp.sum(p3 * gp, axis=0)
                gs = (p3 * (gp - dot[None]) * scale).reshape(G, G).astype(BF16)
                parts.append(nn(k_tr[h * D : (h + 1) * D], gs))
                gk = gk + nn(gs, queries * head_of[h])
                gv = gv + nn(p.astype(BF16), gmixed * head_of[h])
            gq = jnp.transpose(jnp.concatenate(parts, axis=0))
            grads = jnp.concatenate([gq.astype(BF16), gk.astype(BF16), gv.astype(BF16)], axis=1)
            stage[:, eight, :] = nt(grads, wcat).reshape(NF, 8, C)
            acc_qkv[...] += tn(n_s[g], grads)

        gnormed = stage[...].reshape(CP, C).astype(BF16)
        gn_s[chunk, :] = gnormed
        to_time(3, c, gn_s, gn_f)
        acc_gain[...] += jnp.sum((gnormed.astype(F32) * unit_t[chunk, :]).reshape(CP // 8, 8, C), axis=0)

        @pl.when(c == 0)
        def _():
            conv_grad()

        @pl.when(c == 1)
        def _():
            sum_b_send(1, EP, 0, e_r, e_b, e_br)

    for i in range(3):
        for k in range(8):
            lo = max(i * C, k * 48)
            hi = min((i + 1) * C, (k + 1) * 48)
            if lo < hi:
                at = k * LP + lo - k * 48
                l_s[at : at + hi - lo, :] = acc_qkv[lo - i * C : hi - i * C, i * C : (i + 1) * C].astype(BF16)
    total_gain = jnp.sum(acc_gain[...], axis=0, keepdims=True)
    for k in range(8):
        l_s[k * LP + 48 : (k + 1) * LP, :] = jnp.broadcast_to(total_gain, (16, C)).astype(BF16)
    sum_a_send(4, LP, l_s, l_r)
    sum_b_back(2, EP, 0, e_br, e_g)
    conv_out()
    sum_b_send(5, LP, EB, l_r, l_b, l_br)
    sum_a_back(3, EP, 0, e_g, e_f)
    sum_b_back(6, LP, EB, l_br, l_g)

    @pl.loop(0, NC)
    def _(c):
        arrived(3, c, gn_f)
        chunk = rows_of(c * CP, CP)
        unit, inverse = normalize(x_ref[chunk, :].astype(F32))
        gscaled = gn_f[chunk, :].astype(F32) * gain
        first = jnp.mean(gscaled, axis=-1, keepdims=True)
        second = jnp.mean(gscaled * unit, axis=-1, keepdims=True)
        gf_ref[chunk, :] = (gh[chunk, :] + inverse * (gscaled - first - unit * second)).astype(BF16)

    sum_a_back(7, LP, EB, l_g, l_f)
    sum_finish(0, EP, 0, e_r, e_b, e_br, e_f)
    gconv_ref[...] = e_f[: 9 * C, :].astype(F32)
    gout_ref[...] = e_f[9 * C :, :].astype(F32)

    @pl.loop(0, NC)
    def _(c):
        left(0, c, x_ref)
        left(1, c, mix_s)
        left(2, c, gm_s)
        left(3, c, gn_s)

    sum_finish(4, LP, EB, l_r, l_b, l_br, l_f)
    for k in range(8):
        gqkv_ref[k * 48 : (k + 1) * 48, :] = l_f[k * LP : k * LP + 48, :].astype(F32)
    ggain_ref[...] = l_f[48:64, :].astype(F32)[:8]


def on_device(frames, norm_gain, qkv_weight, out_weight, conv_weight, out_grad):
    total_pixels = PIX * NF * NR
    factor = 1.0 / math.sqrt(total_pixels)
    vmem = pl.BlockSpec(memory_space=pltpu.VMEM)
    sds = jax.ShapeDtypeStruct
    full = (PIX, C)
    outs = pl.pallas_call(
        lambda *refs: kernel(factor, *refs),
        out_shape=(
            sds(full, BF16), sds(full, BF16), sds((8, C), F32),
            sds((3 * C, C), F32), sds((C, C), F32), sds((9 * C, C), F32),
        ),
        in_specs=[vmem] * 6,
        out_specs=(vmem,) * 6,
        scratch_shapes=[
            pltpu.VMEM(full, BF16),
            pltpu.VMEM(full, F32),
            pltpu.VMEM((NF, M, C), F32),
            pltpu.VMEM((NC * NG, C, G), BF16),
            pltpu.VMEM((NC * NG, G, C), BF16),
            pltpu.VMEM((NC * NG, G, C), BF16),
            pltpu.VMEM((NC * NG, G, C), BF16),
            pltpu.VMEM((NC * NG * HEADS, G, G), F32),
            pltpu.VMEM(full, BF16),
            pltpu.VMEM(full, BF16),
            pltpu.VMEM(full, BF16),
            pltpu.VMEM(full, BF16),
            pltpu.VMEM(full, BF16),
            pltpu.VMEM(full, BF16),
            pltpu.VMEM((PIX + 2 * W, C), BF16),
            pltpu.VMEM((PIX + 2 * W, C), BF16),
            pltpu.VMEM(full, F32),
            pltpu.VMEM(full, F32),
            pltpu.VMEM(full, F32),
            pltpu.VMEM((ROWS + 2, C, W), BF16),
            pltpu.VMEM((PIX, 3 * C), BF16),
            pltpu.VMEM((C, 3 * C), F32),
            pltpu.VMEM((8, C), F32),
            pltpu.VMEM((C, C), F32),
            pltpu.VMEM((3, C, 3 * C), F32),
            pltpu.VMEM((8 * EP, C), BF16),
            pltpu.VMEM((8 * EP, C), BF16),
            pltpu.VMEM((EP, C), BF16),
            pltpu.VMEM((32 * 16, C), BF16),
            pltpu.VMEM((EP, C), BF16),
            pltpu.VMEM((8 * EP, C), BF16),
            pltpu.VMEM((8 * LP, C), BF16),
            pltpu.VMEM((8 * LP, C), BF16),
            pltpu.VMEM((LP, C), BF16),
            pltpu.VMEM((32 * 16, C), BF16),
            pltpu.VMEM((LP, C), BF16),
            pltpu.VMEM((8 * LP, C), BF16),
            pltpu.SemaphoreType.DMA((4, NC)),
            pltpu.SemaphoreType.DMA((4, NC)),
            pltpu.SemaphoreType.DMA((4,)),
            pltpu.SemaphoreType.DMA((4,)),
            pltpu.SemaphoreType.DMA((8,)),
            pltpu.SemaphoreType.DMA((8,)),
        ],
        compiler_params=pltpu.CompilerParams(
            collective_id=0, has_side_effects=True, vmem_limit_bytes=48 << 20
        ),
        name="block",
    )(
        frames.reshape(full),
        norm_gain.reshape(1, C),
        qkv_weight,
        out_weight,
        conv_weight.reshape(3, 3 * C, C),
        out_grad.reshape(full),
    )
    output, grad_frames, grad_gain, grad_qkv, grad_out, grad_conv = outs
    return (
        output.reshape(frames.shape),
        grad_frames.reshape(frames.shape),
        grad_gain[0],
        grad_qkv.reshape(3, C, C),
        grad_out,
        grad_conv.reshape(3, 3, C, C),
    )


def solution(mesh):
    return jax.shard_map(
        on_device,
        mesh=mesh,
        in_specs=(P("frame", "row", None, None), P(), P(), P(), P(), P("frame", "row", None, None)),
        out_specs=(
            P("frame", "row", None, None),
            P("frame", "row", None, None),
            P(),
            P(),
            P(),
            P(),
        ),
        check_vma=False,
    )
```

time: 676 us -> 102 us (0.15)
  waiting for transfers between devices: 302 us -> 0 us
  Pallas kernels: 0 us -> 91.8 us
  local copies, waits for them, and re-layouts: 88.4 us -> 9.37 us
  starting transfers between devices: 78.3 us -> 0 us
  blocking collectives: 74.6 us -> 0 us
  matrix products: 62.5 us -> 0 us
  other arithmetic: 50.6 us -> 0 us
  between operations: 14.9 us -> 0.66 us
    psum x1 -> x0, waiting for transfers between devices: 247 us -> none  [on_device(): lax.psum((grad_gain, grad_qkv, grad_out, grad_conv), ('frame', 'row'))]
    pallas_call x0 -> x1, Pallas kernels: none -> 91.8 us  [on_device(): pl.pallas_call(lambda *refs: kernel(factor, *refs), out_shape=(sds(full,...]
    psum x1 -> x0, blocking collectives: 74.6 us -> none  [on_device(): lax.psum((grad_gain, grad_qkv, grad_out, grad_conv), ('frame', 'row'))]
    all_to_all x8 -> x0, starting transfers between devices: 57.9 us -> none  [the longest x1 12.9 us: on_device(): lax.all_to_all(local_v, 'frame', split_axis=1, concat_axis=0, tiled=True)]
    dot_general x44 -> x0, matrix products: 57.3 us -> none  [the longest x9 10.6 us: convolve_back(): jnp.dot(slab, weight[row_off, col_off].T, preferred_element_type=jnp.floa...]
    reshape x14 -> x0, local copies, waits for them, and re-layouts: 47.6 us -> none  [the longest x3 18.4 us: project(): return tuple((jnp.dot(flat, qkv_weight[index], preferred_element_type=jnp...]
    all_to_all x8 -> x0, waiting for transfers between devices: 46.9 us -> none  [the longest x1 10.6 us: on_device(): lax.all_to_all(local_q, 'frame', split_axis=1, concat_axis=0, tiled=True)]
    unnamed x4 -> x0, other arithmetic: 35.2 us -> none
  transfers between devices with their start and end apart: 13 -> 0, of which waited for: 9 -> 0; matrix products, arithmetic and copies ran while one was open for 16% -> 0% of each run, Pallas kernels for 0% -> 0%
where the time goes in v1:
time: 102 us
  Pallas kernels  91.8 us (90%)
  local copies, waits for them, and re-layouts  9.37 us (9%)
    pallas_call x1, Pallas kernels, on_device(): pl.pallas_call(lambda *refs: kernel(factor, *refs), out_shape=(sds(full,...  91.8 us
    unnamed x17, local copies, waits for them, and re-layouts  8.86 us

profile of v1, /device:TPU:1, one launch (start us, length us, event | category | flops | bytes accessed | tf_op | source)
XLA Modules:
  0.0 101.8 jit_solution(14956421996792022490)
XLA Ops:
  0.6 0.0 copy-start.5
  0.6 0.6 copy-done.5
  1.3 0.0 copy-start
  1.3 1.0 copy-done
  2.3 0.0 copy-start.1
  2.3 1.0 copy-done.1
  3.3 0.0 copy-start.2
  3.3 1.0 copy-done.2
  4.2 0.0 copy-start.3
  4.2 0.9 copy-done.3
  5.1 0.0 copy-start.4
  5.1 0.8 copy-done.4
  5.9 91.8 %block.1 = (bf16[1536,128]{1,0:T(8,128)(2,1)S(1)}, bf16[1536,128]{1,0:T(8,128)(2,1)S(1)}, f32[8,128]{1,0:T(8,128)S(1)}, f32[384,128]{1,0:T(8,128)S(1)}, f32[128,128]{1,0:T(8,128)S(1)}, /*index=5*/f32[1152,128]{1,0:T(8,128)S(1)}) custom-call(bf16[1536,128]{1,0:T(8,128)(2,1)S(1)} %bitcast.13, f32[1,128]{1,0:T(1,128)S(1)} %bitcast.17, ...), custom_call_target="tpu_custom_call" | custom-call | tf_op jit(solution)/shard_map/block/pallas_call | solution.py:493
  97.7 0.5 slice_bitcast_fusion
  98.2 0.7 copy.17
  98.9 0.7 copy.18
  99.7 0.7 copy.19
  100.3 0.6 copy.20
  101.0 0.8 copy.21
Async XLA Ops:
  0.6 0.7 copy-start.5
  1.3 1.0 copy-start
  2.3 1.0 copy-start.1
  3.3 1.0 copy-start.2
  4.2 0.9 copy-start.3
  5.1 0.8 copy-start.4

commit v2 on v1

v2 whole, which is shorter than its diff:
```python
import math

import jax
import jax.numpy as jnp
from jax import lax
from jax.experimental import pallas as pl
from jax.experimental.pallas import tpu as pltpu
from jax.sharding import PartitionSpec as P

HEADS = 4
EPSILON = 1e-05
MESH = pl.DeviceIdType.MESH
F32 = jnp.float32
BF16 = jnp.bfloat16

NF = 32
NR = 8
C = 128
D = C // HEADS
ROWS = 4
W = 384
PIX = ROWS * W
NC = 3
CP = PIX // NC
M = CP // NF
NG = M // 8
G = 8 * NF
Q = G // 2
LOG2E = math.log2(math.e)

EP = 160
LP = 64
EB = EP // 16
ACT_PIECES = ((0,), (1,), (2,))
OG_PIECES = ((0, 1, 2), (), ())


def nn(a, b):
    return jnp.dot(a, b, preferred_element_type=F32)


def nt(a, b):
    return lax.dot_general(a, b, (((1,), (1,)), ((), ())), preferred_element_type=F32)


def tn(a, b):
    return lax.dot_general(a, b, (((0,), (0,)), ((), ())), preferred_element_type=F32)


def rows_of(start, size):
    return pl.ds(pl.multiple_of(start, size), size)


def normalize(values):
    center = jnp.mean(values, axis=-1, keepdims=True)
    spread = jnp.mean(jnp.square(values - center), axis=-1, keepdims=True)
    inverse = lax.rsqrt(spread + EPSILON)
    return (values - center) * inverse, inverse


def kernel(
    factor,
    x_hbm, gain_hbm, wqkv_hbm, wout_hbm, wconv_hbm, og_hbm,
    out_hbm, gf_hbm, e_f, l_f,
    x_ref, gain_ref, wqkv_ref, wout_ref, wconv_ref,
    xt, unit_t, stage, k_t, v_s, q_s, n_s, probs,
    mix_s, mix_f, gm_s, gm_t, gn_s, gn_f, out_ref, gf_ref,
    ogp, actp, gact, hid, gh, act_t, og_sh,
    acc_qkv, acc_gain, acc_out,
    e_s, e_r, e_b, e_br, e_g,
    l_s, l_r, l_b, l_br, l_g,
    isem, osem, snd, rcv, hsnd, hrcv, wsnd, wrcv,
):
    f = lax.axis_index("frame")
    r = lax.axis_index("row")
    core = lax.rem(f, 2)
    fx = f // 2
    y = r // 2
    zh = lax.rem(r, 2)
    a = y * 2 + core
    q = zh * 16 + fx

    def frame_peer(k):
        return lax.rem(f + k, NF)

    def a_peer(k):
        a2 = lax.rem(a + k, 8)
        return a2, (fx * 2 + lax.rem(a2, 2), (a2 // 2) * 2 + zh)

    def q_device(q2):
        return (lax.rem(q2, 16) * 2 + core, y * 2 + q2 // 16)

    barrier = pltpu.get_barrier_semaphore()

    fetches = [
        pltpu.make_async_copy(src, dst, isem.at[k])
        for k, (src, dst) in enumerate([
            (x_hbm, x_ref), (gain_hbm, gain_ref), (wqkv_hbm, wqkv_ref), (wout_hbm, wout_ref),
            (wconv_hbm, wconv_ref), (og_hbm, ogp.at[pl.ds(W, PIX)]),
        ])
    ]
    for fetch in fetches:
        fetch.start()

    @pl.loop(1, NF, unroll=True)
    def _(k):
        pl.semaphore_signal(barrier, inc=1, device_id=(frame_peer(k), r), device_id_type=MESH)

    @pl.loop(0, 16, unroll=True)
    def _(k):
        pl.semaphore_signal(barrier, inc=1, device_id=(k * 2 + core, y * 2 + 1 - zh), device_id_type=MESH)

    @pl.loop(2, 8, unroll=True)
    def _(k):
        a2 = lax.rem(y * 2 + k, 8)
        pl.semaphore_signal(
            barrier, inc=1, device_id=(fx * 2 + lax.rem(a2, 2), (a2 // 2) * 2 + zh), device_id_type=MESH)

    @pl.when(r > 0)
    def _():
        pl.semaphore_signal(barrier, inc=1, device_id=(f, r - 1), device_id_type=MESH)

    @pl.when(r < NR - 1)
    def _():
        pl.semaphore_signal(barrier, inc=1, device_id=(f, r + 1), device_id_type=MESH)

    col = lax.broadcasted_iota(jnp.int32, (W, C), 0)
    first_col = col == 0
    last_col = col == W - 1

    def after(z):
        return jnp.where(last_col, 0.0, pltpu.roll(z, W - 1, 0))

    def before(z):
        return jnp.where(first_col, 0.0, pltpu.roll(z, 1, 0))

    def shift_row(row):
        here = rows_of(row * W, W)
        own = ogp[here, :]
        wide = own.astype(F32)
        og_sh[here, :] = jnp.concatenate([after(wide).astype(BF16), own, before(wide).astype(BF16)], axis=1)

    def grad_act_row(row):
        total = jnp.zeros((W, 3 * C), F32)
        for i in range(3):
            total = total + nt(ogp[rows_of((row + 2 - i) * W, W), :], wconv_ref[i])
        gact[rows_of(row * W, W), :] = (
            after(total[:, :C]) + total[:, C : 2 * C] + before(total[:, 2 * C :]))

    for fetch in fetches:
        fetch.wait()

    @pl.loop(1, ROWS - 1)
    def _(row):
        grad_act_row(row)

    @pl.loop(1, ROWS + 1)
    def _(row):
        shift_row(row)

    pl.semaphore_wait(barrier, 31 + 16 + 6 + jnp.where(r > 0, 1, 0) + jnp.where(r < NR - 1, 1, 0))

    def to_time(phase, c, src, dst):
        @pl.loop(1, NF, unroll=True)
        def _(k):
            d = frame_peer(k)
            pltpu.make_async_remote_copy(
                src.at[rows_of(c * CP + d * M, M)], dst.at[rows_of(c * CP + f * M, M)],
                snd.at[phase, c], rcv.at[phase, c], device_id=(d, r), device_id_type=MESH,
            ).start()

        own = rows_of(c * CP + f * M, M)
        dst[own, :] = src[own, :]

    def arrived(phase, c, dst):
        view = dst.at[pl.ds(pl.multiple_of(c * CP, M), (NF - 1) * M)]
        pltpu.make_async_copy(view, view, rcv.at[phase, c]).wait()

    def left(phase, c, src):
        view = src.at[pl.ds(pl.multiple_of(c * CP, M), (NF - 1) * M)]
        pltpu.make_async_copy(view, view, snd.at[phase, c]).wait()

    def turn(t):
        return lax.rem(NC + 1 - t, NC)

    @pl.loop(0, NC)
    def _(t):
        to_time(0, turn(t), x_ref, xt)

    def halo_up(buf, s, piece):
        return pltpu.make_async_remote_copy(
            buf.at[pl.ds(W + piece * C, C)], buf.at[pl.ds(5 * W + piece * C, C)],
            hsnd.at[s, 0, piece], hrcv.at[s, 0, piece], device_id=(f, r - 1), device_id_type=MESH)

    def halo_down(buf, s, piece):
        return pltpu.make_async_remote_copy(
            buf.at[pl.ds(4 * W + piece * C, C)], buf.at[pl.ds(piece * C, C)],
            hsnd.at[s, 1, piece], hrcv.at[s, 1, piece], device_id=(f, r + 1), device_id_type=MESH)

    def halo_start(buf, s, pieces):
        @pl.when(r > 0)
        def _():
            for piece in pieces:
                halo_up(buf, s, piece).start()

        @pl.when(r < NR - 1)
        def _():
            for piece in pieces:
                halo_down(buf, s, piece).start()

    edge = jnp.zeros((W, C), BF16)

    @pl.when(r == 0)
    def _():
        ogp[pl.ds(0, W), :] = edge
        actp[pl.ds(0, W), :] = edge

    @pl.when(r == NR - 1)
    def _():
        ogp[pl.ds(5 * W, W), :] = edge
        actp[pl.ds(5 * W, W), :] = edge

    def halo_wait(buf, s):
        @pl.when(r > 0)
        def _():
            for piece in range(3):
                halo_up(buf, s, piece).wait_send()
                halo_down(buf, s, piece).wait_recv()

        @pl.when(r < NR - 1)
        def _():
            for piece in range(3):
                halo_down(buf, s, piece).wait_send()
                halo_up(buf, s, piece).wait_recv()

    gain = gain_ref[...]
    wcat = jnp.concatenate([wqkv_ref[0], wqkv_ref[1], wqkv_ref[2]], axis=1)
    scale = D ** (-0.5)
    sub = lax.broadcasted_iota(jnp.int32, (8, 2 * Q), 0)
    lane = lax.broadcasted_iota(jnp.int32, (8, 2 * Q), 1)
    diag = (lax.rem(sub, 4) == lax.rem(lane, 4)).astype(F32)
    first_half = lax.broadcasted_iota(jnp.int32, (NF // 2, 8, C), 1) < 4

    def quads(rows):
        lo, hi = rows[: NF // 2], rows[NF // 2 :]
        one = jnp.where(first_half, lo, pltpu.roll(hi, 4, 1)).reshape(Q, C)
        two = jnp.where(first_half, pltpu.roll(lo, 4, 1), hi).reshape(Q, C)
        return jnp.concatenate([one, two], axis=0).astype(BF16)

    def from_quads(rows):
        one = rows[:Q].reshape(NF // 2, 8, C)
        two = rows[Q:].reshape(NF // 2, 8, C)
        lo = jnp.where(first_half, one, pltpu.roll(two, 4, 1))
        hi = jnp.where(first_half, pltpu.roll(one, 4, 1), two)
        return jnp.concatenate([lo, hi], axis=0)

    def two_heads(tr, pair):
        wide = []
        for h in (2 * pair, 2 * pair + 1):
            pieces = [jnp.zeros((h * D, Q), BF16)] if h else []
            pieces.append(tr[h * D : (h + 1) * D])
            if h < HEADS - 1:
                pieces.append(jnp.zeros((C - (h + 1) * D, Q), BF16))
            wide.append(jnp.concatenate(pieces, axis=0))
        return jnp.concatenate(wide, axis=1)

    def by_head(rows):
        return jnp.concatenate([rows * head_of[h] for h in range(HEADS)], axis=0)

    chan = lax.broadcasted_iota(jnp.int32, (1, C), 1) // D
    head_of = [(chan == h).astype(BF16) for h in range(HEADS)]

    acc_qkv[...] = jnp.zeros_like(acc_qkv)
    acc_gain[...] = jnp.zeros_like(acc_gain)
    acc_out[...] = jnp.zeros_like(acc_out)

    @pl.loop(0, NC)
    def _(t):
        c = turn(t)
        arrived(0, c, xt)

        @pl.when(t == 0)
        def _():
            halo_start(ogp, 0, OG_PIECES[0])

        chunk = rows_of(c * CP, CP)
        unit, _ = normalize(xt[chunk, :].astype(F32))
        unit_t[chunk, :] = unit
        stage[...] = (unit * gain).reshape(NF, M, C)

        @pl.loop(0, NG)
        def _(j):
            g = c * NG + j
            eight = pl.ds(pl.multiple_of(j * 8, 8), 8)
            normed = quads(stage[:, eight, :])
            n_s[g] = normed
            qkv = nn(normed, wcat).astype(BF16)
            queries, keys, values = qkv[:, :C], qkv[:, C : 2 * C], qkv[:, 2 * C :]
            q_s[g] = queries
            v_s[g] = values
            q_tr = jnp.transpose(queries)
            k_tr = jnp.transpose(keys)
            v_tr = jnp.transpose(values)
            k_t[g] = k_tr
            mixed = []
            for b in range(2):
                at = slice(b * Q, (b + 1) * Q)
                parts = []
                for pair in range(HEADS // 2):
                    s = nn(keys[at], two_heads(q_tr[:, at], pair)).reshape(Q // 8, 8, 2 * Q)
                    top = jnp.max(s, axis=0)
                    top = jnp.maximum(top, pltpu.roll(top, 4, 0))
                    e = jnp.exp2((s - top[None]) * (scale * LOG2E))
                    below = jnp.sum(e, axis=0)
                    inv = diag / (below + pltpu.roll(below, 4, 0))
                    p = (e * inv[None]).reshape(Q, 2 * Q)
                    probs[(g * 2 + b) * 2 + pair] = p
                    pb = p.astype(BF16)
                    for k in range(2):
                        h = 2 * pair + k
                        parts.append(nn(v_tr[h * D : (h + 1) * D, at], pb[:, k * Q : (k + 1) * Q]))
                mixed.append(jnp.concatenate(parts, axis=0))
            stage[:, eight, :] = from_quads(jnp.transpose(jnp.concatenate(mixed, axis=1)))

        mix_s[chunk, :] = stage[...].reshape(CP, C).astype(BF16)
        to_time(1, c, mix_s, mix_f)

        for late in (1, 2):
            if OG_PIECES[late]:
                @pl.when(t == late - 1)
                def _(late=late):
                    halo_start(ogp, 0, OG_PIECES[late])

    def middle(c):
        arrived(1, c, mix_f)
        chunk = pl.ds(c * CP, CP)
        mixed = mix_f[chunk, :]
        hidden = x_ref[chunk, :].astype(F32) + nn(mixed, wout_ref[...])
        sigma = 1.0 / (1.0 + jnp.exp(-hidden))
        act = (hidden * sigma).astype(BF16)
        ghidden = (ogp[pl.ds(W + c * CP, CP), :].astype(F32)
                   + gact[chunk, :] * sigma * (1.0 + hidden * (1.0 - sigma)))
        ghb = ghidden.astype(BF16)
        gm_s[chunk, :] = nt(ghb, wout_ref[...]).astype(BF16)
        to_time(2, c, gm_s, gm_t)
        hid[chunk, :] = hidden
        actp[pl.ds(W + c * CP, CP), :] = act
        gh[chunk, :] = ghidden
        acc_out[...] += tn(mixed, ghb)
        act_t[:, c * CP : (c + 1) * CP] = jnp.transpose(act)

    middle(1)
    halo_wait(ogp, 0)

    @pl.loop(0, 2)
    def _(k):
        grad_act_row(k * (ROWS - 1))

    middle(0)
    middle(2)

    def sum_a_send(s, size, src, dst):
        @pl.loop(1, 8)
        def _(k):
            a2, dev = a_peer(k)
            pltpu.make_async_remote_copy(
                src.at[rows_of(a2 * size, size)], dst.at[rows_of(a * size, size)],
                wsnd.at[s], wrcv.at[s], device_id=dev, device_id_type=MESH).start()

        own = rows_of(a * size, size)
        dst[own, :] = src[own, :]

    def sum_b_send(s, size, base, src, mid, dst):
        view = src.at[pl.ds(0, 7 * size)]
        pltpu.make_async_copy(view, view, wrcv.at[s - 1]).wait()
        total = src[pl.ds(0, size), :].astype(F32)
        for k in range(1, 8):
            total = total + src[pl.ds(k * size, size), :].astype(F32)
        mid[...] = total.astype(BF16)

        @pl.loop(0, size // 16)
        def _(o):
            owner = 2 * (base + o)

            @pl.when(owner != q)
            def _():
                pltpu.make_async_remote_copy(
                    mid.at[rows_of(o * 16, 16)], dst.at[rows_of(q * 16, 16)],
                    wsnd.at[s], wrcv.at[s], device_id=q_device(owner), device_id_type=MESH).start()

            @pl.when(owner == q)
            def _():
                dst[rows_of(q * 16, 16), :] = mid[rows_of(o * 16, 16), :]

    def owns(size, base):
        return jnp.logical_and(
            lax.rem(q, 2) == 0, jnp.logical_and(q >= 2 * base, q < 2 * base + size // 8))

    def sum_b_back(s, size, base, src, dst):
        @pl.when(owns(size, base))
        def _():
            view = src.at[pl.ds(0, 31 * 16)]
            pltpu.make_async_copy(view, view, wrcv.at[s - 1]).wait()
            total = jnp.sum(src[...].astype(F32).reshape(32, 16, C), axis=0) * factor
            mine = rows_of((q // 2 - base) * 16, 16)
            dst[mine, :] = total.astype(BF16)

            @pl.loop(1, 32)
            def _(k):
                pltpu.make_async_remote_copy(
                    dst.at[mine], dst.at[mine], wsnd.at[s], wrcv.at[s],
                    device_id=q_device(lax.rem(q + k, 32)), device_id_type=MESH).start()

    def sum_a_back(s, size, base, src, dst):
        nblock = size // 16

        @pl.when(owns(size, base))
        def _():
            view = src.at[pl.ds(0, (nblock - 1) * 16)]
            pltpu.make_async_copy(view, view, wrcv.at[s - 1]).wait()

        @pl.when(jnp.logical_not(owns(size, base)))
        def _():
            view = src.at[pl.ds(0, nblock * 16)]
            pltpu.make_async_copy(view, view, wrcv.at[s - 1]).wait()

        own = rows_of(a * size, size)

        @pl.loop(1, 8)
        def _(k):
            pltpu.make_async_remote_copy(
                src, dst.at[own], wsnd.at[s], wrcv.at[s], device_id=a_peer(k)[1], device_id_type=MESH).start()

        pltpu.make_async_copy(src, dst.at[own], osem.at[s // 4]).start()

    def sum_finish(s, size, base, src, mid, back, total, dst):
        own = rows_of(a * size, size)
        pltpu.make_async_copy(total, dst.at[own], osem.at[s // 4]).wait()
        view = dst.at[pl.ds(0, 7 * size)]
        pltpu.make_async_copy(view, view, wrcv.at[s + 3]).wait()
        sent = src.at[pl.ds(0, 7 * size)]
        pltpu.make_async_copy(sent, sent, wsnd.at[s]).wait()
        nblock = size // 16

        @pl.when(owns(size, base))
        def _():
            few = mid.at[pl.ds(0, (nblock - 1) * 16)]
            pltpu.make_async_copy(few, few, wsnd.at[s + 1]).wait()
            many = back.at[pl.ds(0, 31 * 16)]
            pltpu.make_async_copy(many, many, wsnd.at[s + 2]).wait()

        @pl.when(jnp.logical_not(owns(size, base)))
        def _():
            few = mid.at[pl.ds(0, nblock * 16)]
            pltpu.make_async_copy(few, few, wsnd.at[s + 1]).wait()

        pltpu.make_async_copy(view, view, wsnd.at[s + 3]).wait()

    @pl.loop(0, 2)
    def _(k):
        shift_row(k * (ROWS + 1))

    for i in range(3):
        grad = nn(act_t[...], og_sh[(2 - i) * W : (2 - i) * W + PIX, :])
        for j in range(3):
            at = (3 * i + j) * C
            e_s[at : at + C, :] = grad[:, j * C : (j + 1) * C].astype(BF16)
    e_s[9 * C : 10 * C, :] = acc_out[...].astype(BF16)
    sum_a_send(0, EP, e_s, e_r)

    def conv_row(row):
        total = jnp.zeros((W, 3 * C), F32)
        for i in range(3):
            wide = jnp.concatenate([wconv_ref[i, j * C : (j + 1) * C, :] for j in range(3)], axis=1)
            total = total + nn(actp[rows_of((row + i) * W, W), :], wide)
        here = rows_of(row * W, W)
        conv = before(total[:, :C]) + total[:, C : 2 * C] + after(total[:, 2 * C :])
        out_ref[here, :] = (hid[here, :] + conv).astype(BF16)

    @pl.loop(0, NC)
    def _(t):
        c = turn(t)
        arrived(2, c, gm_t)
        chunk = rows_of(c * CP, CP)
        stage[...] = gm_t[chunk, :].astype(F32).reshape(NF, M, C)

        @pl.loop(0, NG)
        def _(j):
            g = c * NG + j
            eight = pl.ds(pl.multiple_of(j * 8, 8), 8)
            gmixed = quads(stage[:, eight, :])
            gm_tr = jnp.transpose(gmixed)
            queries, values, k_tr = q_s[g], v_s[g], k_t[g]
            gqs, gks, gvs = [], [], []
            for b in range(2):
                at = slice(b * Q, (b + 1) * Q)
                parts, scores, weights = [], [], []
                for pair in range(HEADS // 2):
                    gp = nn(values[at], two_heads(gm_tr[:, at], pair)).reshape(Q // 8, 8, 2 * Q)
                    p = probs[(g * 2 + b) * 2 + pair]
                    p3 = p.reshape(Q // 8, 8, 2 * Q)
                    dot = jnp.sum(p3 * gp, axis=0)
                    dot = dot + pltpu.roll(dot, 4, 0)
                    gs = (p3 * (gp - dot[None]) * scale).reshape(Q, 2 * Q).astype(BF16)
                    for k in range(2):
                        h = 2 * pair + k
                        parts.append(nn(k_tr[h * D : (h + 1) * D, at], gs[:, k * Q : (k + 1) * Q]))
                    scores.append(gs)
                    weights.append(p.astype(BF16))
                gqs.append(jnp.concatenate(parts, axis=0))
                gks.append(nn(jnp.concatenate(scores, axis=1), by_head(queries[at])))
                gvs.append(nn(jnp.concatenate(weights, axis=1), by_head(gmixed[at])))
            gq = jnp.transpose(jnp.concatenate(gqs, axis=1))
            gk, gv = jnp.concatenate(gks, axis=0), jnp.concatenate(gvs, axis=0)
            grads = jnp.concatenate([gq.astype(BF16), gk.astype(BF16), gv.astype(BF16)], axis=1)
            stage[:, eight, :] = from_quads(nt(grads, wcat))
            acc_qkv[...] += tn(n_s[g], grads)

        gnormed = stage[...].reshape(CP, C).astype(BF16)
        gn_s[chunk, :] = gnormed
        to_time(3, c, gn_s, gn_f)
        acc_gain[...] += jnp.sum((gnormed.astype(F32) * unit_t[chunk, :]).reshape(CP // 8, 8, C), axis=0)

        @pl.when(t == 1)
        def _():
            sum_b_send(1, EP, 0, e_r, e_b, e_br)

    for i in range(3):
        for k in range(8):
            lo = max(i * C, k * 48)
            hi = min((i + 1) * C, (k + 1) * 48)
            if lo < hi:
                at = k * LP + lo - k * 48
                l_s[at : at + hi - lo, :] = acc_qkv[lo - i * C : hi - i * C, i * C : (i + 1) * C].astype(BF16)
    total_gain = jnp.sum(acc_gain[...], axis=0, keepdims=True)
    for k in range(8):
        l_s[k * LP + 48 : (k + 1) * LP, :] = jnp.broadcast_to(total_gain, (16, C)).astype(BF16)
    sum_a_send(4, LP, l_s, l_r)
    halo_start(actp, 1, ACT_PIECES[0])
    sum_b_back(2, EP, 0, e_br, e_g)

    def put_out(k, at, size):
        rows = pl.ds(at, size)
        return pltpu.make_async_copy(out_ref.at[rows], out_hbm.at[rows], osem.at[2 + k])

    @pl.loop(1, ROWS - 1)
    def _(row):
        conv_row(row)

    put_out(0, W, 2 * W).start()
    sum_b_send(5, LP, EB, l_r, l_b, l_br)
    halo_start(actp, 1, ACT_PIECES[1])
    sum_a_back(3, EP, 0, e_g, e_f)

    def put_gf(c):
        chunk = rows_of(c * CP, CP)
        return pltpu.make_async_copy(gf_ref.at[chunk], gf_hbm.at[chunk], osem.at[5 + c])

    def grad_frames(c):
        arrived(3, c, gn_f)
        chunk = rows_of(c * CP, CP)
        unit, inverse = normalize(x_ref[chunk, :].astype(F32))
        gscaled = gn_f[chunk, :].astype(F32) * gain
        first = jnp.mean(gscaled, axis=-1, keepdims=True)
        second = jnp.mean(gscaled * unit, axis=-1, keepdims=True)
        gf_ref[chunk, :] = (gh[chunk, :] + inverse * (gscaled - first - unit * second)).astype(BF16)
        put_gf(c).start()

    grad_frames(1)
    grad_frames(0)
    sum_b_back(6, LP, EB, l_br, l_g)
    halo_start(actp, 1, ACT_PIECES[2])
    grad_frames(2)
    sum_a_back(7, LP, EB, l_g, l_f)
    halo_wait(actp, 1)

    @pl.loop(0, 2)
    def _(k):
        conv_row(k * (ROWS - 1))

    put_out(1, 0, W).start()
    put_out(2, 3 * W, W).start()
    sum_finish(0, EP, 0, e_r, e_b, e_br, e_g, e_f)

    @pl.loop(0, NC)
    def _(c):
        left(0, c, x_ref)
        left(1, c, mix_s)
        left(2, c, gm_s)
        left(3, c, gn_s)

    for c in range(NC):
        put_gf(c).wait()
    put_out(0, W, 2 * W).wait()
    put_out(1, 0, W).wait()
    put_out(2, 3 * W, W).wait()
    sum_finish(4, LP, EB, l_r, l_b, l_br, l_g, l_f)


def finish(
    out_s, gf_s, e_h, l_h, out_h, gf_h, gain_h, qkv_h, gout_h, conv_h,
    gain, qkv, gout, conv, e_v, l_v, out_v, gf_v, sem,
):
    def put(k, src, dst):
        copy = pltpu.make_async_copy(src, dst, sem.at[k])
        copy.start()
        return copy

    early, late = put(6, e_h, e_v), put(7, l_h, l_v)
    first, second = put(8, out_s, out_v), put(9, gf_s, gf_v)
    copies = []
    early.wait()
    conv[...] = e_v[: 9 * C, :].astype(F32)
    copies.append(put(2, conv, conv_h))
    gout[...] = e_v[9 * C :, :].astype(F32)
    copies.append(put(3, gout, gout_h))
    first.wait()
    copies.append(put(0, out_v, out_h))
    second.wait()
    copies.append(put(1, gf_v, gf_h))
    late.wait()
    for k in range(8):
        qkv[k * 48 : (k + 1) * 48, :] = l_v[k * LP : k * LP + 48, :].astype(F32)
    copies.append(put(4, qkv, qkv_h))
    gain[...] = l_v[48:64, :].astype(F32)[:1]
    copies.append(put(5, gain, gain_h))
    for copy in copies:
        copy.wait()


def on_device(frames, norm_gain, qkv_weight, out_weight, conv_weight, out_grad):
    total_pixels = PIX * NF * NR
    factor = 1.0 / math.sqrt(total_pixels)
    hbm = pl.BlockSpec(memory_space=pltpu.HBM)
    sds = jax.ShapeDtypeStruct
    full = (PIX, C)
    parts = pl.pallas_call(
        lambda *refs: kernel(factor, *refs),
        out_shape=(sds(full, BF16), sds(full, BF16), sds((8 * EP, C), BF16), sds((8 * LP, C), BF16)),
        in_specs=[hbm] * 6,
        out_specs=(hbm,) * 4,
        scratch_shapes=[
            pltpu.VMEM(full, BF16),
            pltpu.VMEM((1, C), F32),
            pltpu.VMEM((3, C, C), BF16),
            pltpu.VMEM((C, C), BF16),
            pltpu.VMEM((3, 3 * C, C), BF16),
            pltpu.VMEM(full, BF16),
            pltpu.VMEM(full, F32),
            pltpu.VMEM((NF, M, C), F32),
            pltpu.VMEM((NC * NG, C, G), BF16),
            pltpu.VMEM((NC * NG, G, C), BF16),
            pltpu.VMEM((NC * NG, G, C), BF16),
            pltpu.VMEM((NC * NG, G, C), BF16),
            pltpu.VMEM((NC * NG * HEADS, Q, 2 * Q), F32),
            pltpu.VMEM(full, BF16),
            pltpu.VMEM(full, BF16),
            pltpu.VMEM(full, BF16),
            pltpu.VMEM(full, BF16),
            pltpu.VMEM(full, BF16),
            pltpu.VMEM(full, BF16),
            pltpu.VMEM(full, BF16),
            pltpu.VMEM(full, BF16),
            pltpu.VMEM((PIX + 2 * W, C), BF16),
            pltpu.VMEM((PIX + 2 * W, C), BF16),
            pltpu.VMEM(full, F32),
            pltpu.VMEM(full, F32),
            pltpu.VMEM(full, F32),
            pltpu.VMEM((C, PIX), BF16),
            pltpu.VMEM((PIX + 2 * W, 3 * C), BF16),
            pltpu.VMEM((C, 3 * C), F32),
            pltpu.VMEM((8, C), F32),
            pltpu.VMEM((C, C), F32),
            pltpu.VMEM((8 * EP, C), BF16),
            pltpu.VMEM((8 * EP, C), BF16),
            pltpu.VMEM((EP, C), BF16),
            pltpu.VMEM((32 * 16, C), BF16),
            pltpu.VMEM((EP, C), BF16),
            pltpu.VMEM((8 * LP, C), BF16),
            pltpu.VMEM((8 * LP, C), BF16),
            pltpu.VMEM((LP, C), BF16),
            pltpu.VMEM((32 * 16, C), BF16),
            pltpu.VMEM((LP, C), BF16),
            pltpu.SemaphoreType.DMA((6,)),
            pltpu.SemaphoreType.DMA((8,)),
            pltpu.SemaphoreType.DMA((4, NC)),
            pltpu.SemaphoreType.DMA((4, NC)),
            pltpu.SemaphoreType.DMA((2, 2, 3)),
            pltpu.SemaphoreType.DMA((2, 2, 3)),
            pltpu.SemaphoreType.DMA((8,)),
            pltpu.SemaphoreType.DMA((8,)),
        ],
        compiler_params=pltpu.CompilerParams(
            collective_id=0, has_side_effects=True, vmem_limit_bytes=60 << 20
        ),
        name="block",
    )(
        frames.reshape(full),
        norm_gain.reshape(1, C),
        qkv_weight,
        out_weight,
        conv_weight.reshape(3, 3 * C, C),
        out_grad.reshape(full),
    )
    sizes = (sds(full, BF16), sds(full, BF16), sds((1, C), F32),
             sds((3 * C, C), F32), sds((C, C), F32), sds((9 * C, C), F32))
    outs = pl.pallas_call(
        finish,
        out_shape=sizes,
        in_specs=[hbm] * 4,
        out_specs=(hbm,) * 6,
        scratch_shapes=[pltpu.VMEM(s.shape, F32) for s in sizes[2:]] + [
            pltpu.VMEM((8 * EP, C), BF16), pltpu.VMEM((8 * LP, C), BF16),
            pltpu.VMEM(full, BF16), pltpu.VMEM(full, BF16), pltpu.SemaphoreType.DMA((10,))],
        compiler_params=pltpu.CompilerParams(vmem_limit_bytes=60 << 20),
        name="finish",
    )(*parts)
    output, grad_frames, grad_gain, grad_qkv, grad_out, grad_conv = outs
    return (
        output.reshape(frames.shape),
        grad_frames.reshape(frames.shape),
        grad_gain.reshape(C),
        grad_qkv.reshape(3, C, C),
        grad_out,
        grad_conv.reshape(3, 3, C, C),
    )


def solution(mesh):
    return jax.shard_map(
        on_device,
        mesh=mesh,
        in_specs=(P("frame", "row", None, None), P(), P(), P(), P(), P("frame", "row", None, None)),
        out_specs=(
            P("frame", "row", None, None),
            P("frame", "row", None, None),
            P(),
            P(),
            P(),
            P(),
        ),
        check_vma=False,
    )
```

time: 102 us -> 90.4 us (0.89)
  local copies, waits for them, and re-layouts: 9.37 us -> 0 us
  Pallas kernels: 91.8 us -> 89.7 us
    unnamed x17 -> x0, local copies, waits for them, and re-layouts: 8.86 us -> none
    pallas_call x1, Pallas kernels: 91.8 us -> 87.4 us  [on_device(): pl.pallas_call(lambda *refs: kernel(factor, *refs), out_shape=(sds(full,...]
    pallas_call x0 -> x1, Pallas kernels: none -> 2.25 us  [on_device(): pl.pallas_call(finish, out_shape=sizes, in_specs=[hbm] * 4, out_specs=(hb...]
where the time goes in v2:
time: 90.4 us; the launch traced here: 90.3 us
  Pallas kernels  89.7 us (99%)
    pallas_call x1, Pallas kernels, on_device(): pl.pallas_call(lambda *refs: kernel(factor, *refs), out_shape=(sds(full,...  87.4 us
    pallas_call x1, Pallas kernels, on_device(): pl.pallas_call(finish, out_shape=sizes, in_specs=[hbm] * 4, out_specs=(hb...  2.25 us

profile of v2, /device:TPU:1, one launch (start us, length us, event | category | flops | bytes accessed | tf_op | source)
XLA Modules:
  0.0 90.3 jit_solution(3070985601109874233)
XLA Ops:
  0.6 87.4 %block.1 = (bf16[1536,128]{1,0:T(8,128)(2,1)}, bf16[1536,128]{1,0:T(8,128)(2,1)}, bf16[1280,128]{1,0:T(8,128)(2,1)}, bf16[512,128]{1,0:T(8,128)(2,1)}) custom-call(bf16[1536,128]{1,0:T(8,128)(2,1)} %bitcast.9, f32[1,128]{1,0:T(1,128)} %bitcast.12, bf16[3,128,128]{2,1,0:T(8,128)(2,1)} %refs_2_.1, bf16[128,128]{1,0:T(8,128)(2,1)} %refs_3_.1, ...), custom_call_target="tpu_custom_call" | custom-call | tf_op jit(solution)/shard_map/block/pallas_call | solution.py:637
  88.1 2.3 %finish.1 = (bf16[1536,128]{1,0:T(8,128)(2,1)}, bf16[1536,128]{1,0:T(8,128)(2,1)}, f32[1,128]{1,0:T(1,128)}, f32[384,128]{1,0:T(8,128)}, f32[128,128]{1,0:T(8,128)}, /*index=5*/f32[1152,128]{1,0:T(8,128)}) custom-call(bf16[1536,128]{1,0:T(8,128)(2,1)} %get-tuple-element.16.out_s, bf16[1536,128]{1,0:T(8,128)(2,1)} %get-tuple-element.17.gf_s, ...), custom_call_target="tpu_custom_call" | custom-call | tf_op jit(solution)/shard_map/finish/pallas_call | solution.py:707

commit v3 on v2

--- a/solution.py
+++ b/solution.py
@@ -31,7 +31,7 @@
 EP = 160
 LP = 64
 EB = EP // 16
-ACT_PIECES = ((0,), (1,), (2,))
+ACT_PIECES = ((0, 1), (2,), ())
 OG_PIECES = ((0, 1, 2), (), ())
 
 
@@ -466,7 +466,6 @@
             at = (3 * i + j) * C
             e_s[at : at + C, :] = grad[:, j * C : (j + 1) * C].astype(BF16)
     e_s[9 * C : 10 * C, :] = acc_out[...].astype(BF16)
-    sum_a_send(0, EP, e_s, e_r)
 
     def conv_row(row):
         total = jnp.zeros((W, 3 * C), F32)
@@ -519,11 +518,12 @@
         gnormed = stage[...].reshape(CP, C).astype(BF16)
         gn_s[chunk, :] = gnormed
         to_time(3, c, gn_s, gn_f)
+        @pl.when(t == 0)
+        def _():
+            sum_a_send(0, EP, e_s, e_r)
+
         acc_gain[...] += jnp.sum((gnormed.astype(F32) * unit_t[chunk, :]).reshape(CP // 8, 8, C), axis=0)
 
-        @pl.when(t == 1)
-        def _():
-            sum_b_send(1, EP, 0, e_r, e_b, e_br)
 
     for i in range(3):
         for k in range(8):
@@ -537,7 +537,6 @@
         l_s[k * LP + 48 : (k + 1) * LP, :] = jnp.broadcast_to(total_gain, (16, C)).astype(BF16)
     sum_a_send(4, LP, l_s, l_r)
     halo_start(actp, 1, ACT_PIECES[0])
-    sum_b_back(2, EP, 0, e_br, e_g)
 
     def put_out(k, at, size):
         rows = pl.ds(at, size)
@@ -549,8 +548,8 @@
 
     put_out(0, W, 2 * W).start()
     sum_b_send(5, LP, EB, l_r, l_b, l_br)
+    sum_b_send(1, EP, 0, e_r, e_b, e_br)
     halo_start(actp, 1, ACT_PIECES[1])
-    sum_a_back(3, EP, 0, e_g, e_f)
 
     def put_gf(c):
         chunk = rows_of(c * CP, CP)
@@ -569,9 +568,11 @@
     grad_frames(1)
     grad_frames(0)
     sum_b_back(6, LP, EB, l_br, l_g)
+    sum_b_back(2, EP, 0, e_br, e_g)
     halo_start(actp, 1, ACT_PIECES[2])
     grad_frames(2)
     sum_a_back(7, LP, EB, l_g, l_f)
+    sum_a_back(3, EP, 0, e_g, e_f)
     halo_wait(actp, 1)
 
     @pl.loop(0, 2)

time: 90.4 us -> 87.9 us (0.972)
  Pallas kernels: 89.7 us -> 87.1 us
    pallas_call x1, Pallas kernels: 87.4 us -> 84.9 us  [on_device(): pl.pallas_call(lambda *refs: kernel(factor, *refs), out_shape=(sds(full,...]
where the time goes in v3:
time: 87.9 us; the launch traced here: 87.8 us
  Pallas kernels  87.1 us (99%)
    pallas_call x1, Pallas kernels, on_device(): pl.pallas_call(lambda *refs: kernel(factor, *refs), out_shape=(sds(full,...  84.9 us
    pallas_call x1, Pallas kernels, on_device(): pl.pallas_call(finish, out_shape=sizes, in_specs=[hbm] * 4, out_specs=(hb...  2.25 us

profile of v3, /device:TPU:1, one launch (start us, length us, event | category | flops | bytes accessed | tf_op | source)
XLA Modules:
  0.0 87.8 jit_solution(5321703641675324996)
XLA Ops:
  0.6 84.9 %block.1 = (bf16[1536,128]{1,0:T(8,128)(2,1)}, bf16[1536,128]{1,0:T(8,128)(2,1)}, bf16[1280,128]{1,0:T(8,128)(2,1)}, bf16[512,128]{1,0:T(8,128)(2,1)}) custom-call(bf16[1536,128]{1,0:T(8,128)(2,1)} %bitcast.9, f32[1,128]{1,0:T(1,128)} %bitcast.12, bf16[3,128,128]{2,1,0:T(8,128)(2,1)} %refs_2_.1, bf16[128,128]{1,0:T(8,128)(2,1)} %refs_3_.1, ...), custom_call_target="tpu_custom_call" | custom-call | tf_op jit(solution)/shard_map/block/pallas_call | solution.py:638
  85.5 2.3 %finish.1 = (bf16[1536,128]{1,0:T(8,128)(2,1)}, bf16[1536,128]{1,0:T(8,128)(2,1)}, f32[1,128]{1,0:T(1,128)}, f32[384,128]{1,0:T(8,128)}, f32[128,128]{1,0:T(8,128)}, /*index=5*/f32[1152,128]{1,0:T(8,128)}) custom-call(bf16[1536,128]{1,0:T(8,128)(2,1)} %get-tuple-element.16.out_s, bf16[1536,128]{1,0:T(8,128)(2,1)} %get-tuple-element.17.gf_s, ...), custom_call_target="tpu_custom_call" | custom-call | tf_op jit(solution)/shard_map/finish/pallas_call | solution.py:708

commit v4 on v3

--- a/solution.py
+++ b/solution.py
@@ -32,7 +32,7 @@
 LP = 64
 EB = EP // 16
 ACT_PIECES = ((0, 1), (2,), ())
-OG_PIECES = ((0, 1, 2), (), ())
+OG_PIECES = ((), (0, 1, 2), ())
 
 
 def nn(a, b):
@@ -547,10 +547,6 @@
         conv_row(row)
 
     put_out(0, W, 2 * W).start()
-    sum_b_send(5, LP, EB, l_r, l_b, l_br)
-    sum_b_send(1, EP, 0, e_r, e_b, e_br)
-    halo_start(actp, 1, ACT_PIECES[1])
-
     def put_gf(c):
         chunk = rows_of(c * CP, CP)
         return pltpu.make_async_copy(gf_ref.at[chunk], gf_hbm.at[chunk], osem.at[5 + c])
@@ -566,6 +562,10 @@
         put_gf(c).start()
 
     grad_frames(1)
+    sum_b_send(5, LP, EB, l_r, l_b, l_br)
+    sum_b_send(1, EP, 0, e_r, e_b, e_br)
+    halo_start(actp, 1, ACT_PIECES[1])
+
     grad_frames(0)
     sum_b_back(6, LP, EB, l_br, l_g)
     sum_b_back(2, EP, 0, e_br, e_g)

time: 87.9 us -> 86.5 us (0.984)
  Pallas kernels: 87.1 us -> 85.7 us
    pallas_call x1, Pallas kernels: 84.9 us -> 83.4 us  [on_device(): pl.pallas_call(lambda *refs: kernel(factor, *refs), out_shape=(sds(full,...]
where the time goes in v4:
time: 86.5 us; the launch traced here: 86.3 us
  Pallas kernels  85.7 us (99%)
    pallas_call x1, Pallas kernels, on_device(): pl.pallas_call(lambda *refs: kernel(factor, *refs), out_shape=(sds(full,...  83.4 us
    pallas_call x1, Pallas kernels, on_device(): pl.pallas_call(finish, out_shape=sizes, in_specs=[hbm] * 4, out_specs=(hb...  2.25 us

profile of v4, /device:TPU:1, one launch (start us, length us, event | category | flops | bytes accessed | tf_op | source)
XLA Modules:
  0.0 86.3 jit_solution(17399440787130745716)
XLA Ops:
  0.6 83.4 %block.1 = (bf16[1536,128]{1,0:T(8,128)(2,1)}, bf16[1536,128]{1,0:T(8,128)(2,1)}, bf16[1280,128]{1,0:T(8,128)(2,1)}, bf16[512,128]{1,0:T(8,128)(2,1)}) custom-call(bf16[1536,128]{1,0:T(8,128)(2,1)} %bitcast.9, f32[1,128]{1,0:T(1,128)} %bitcast.12, bf16[3,128,128]{2,1,0:T(8,128)(2,1)} %refs_2_.1, bf16[128,128]{1,0:T(8,128)(2,1)} %refs_3_.1, ...), custom_call_target="tpu_custom_call" | custom-call | tf_op jit(solution)/shard_map/block/pallas_call | solution.py:638
  84.1 2.3 %finish.1 = (bf16[1536,128]{1,0:T(8,128)(2,1)}, bf16[1536,128]{1,0:T(8,128)(2,1)}, f32[1,128]{1,0:T(1,128)}, f32[384,128]{1,0:T(8,128)}, f32[128,128]{1,0:T(8,128)}, /*index=5*/f32[1152,128]{1,0:T(8,128)}) custom-call(bf16[1536,128]{1,0:T(8,128)(2,1)} %get-tuple-element.16.out_s, bf16[1536,128]{1,0:T(8,128)(2,1)} %get-tuple-element.17.gf_s, ...), custom_call_target="tpu_custom_call" | custom-call | tf_op jit(solution)/shard_map/finish/pallas_call | solution.py:708

commit v5 on v4

--- a/solution.py
+++ b/solution.py
@@ -32,7 +32,7 @@
 LP = 64
 EB = EP // 16
 ACT_PIECES = ((0, 1), (2,), ())
-OG_PIECES = ((), (0, 1, 2), ())
+OG_PIECES = ((), (0, 1), (2,))
 
 
 def nn(a, b):

time: 86.5 us -> 86.8 us (level)
  no operation moved by 1% of the time
where the time goes in v5:
time: 86.8 us; the launch traced here: 86.7 us
  Pallas kernels  86 us (99%)
    pallas_call x1, Pallas kernels, on_device(): pl.pallas_call(lambda *refs: kernel(factor, *refs), out_shape=(sds(full,...  83.8 us
    pallas_call x1, Pallas kernels, on_device(): pl.pallas_call(finish, out_shape=sizes, in_specs=[hbm] * 4, out_specs=(hb...  2.25 us

profile of v5, /device:TPU:1, one launch (start us, length us, event | category | flops | bytes accessed | tf_op | source)
XLA Modules:
  0.0 86.7 jit_solution(16186994948818892294)
XLA Ops:
  0.6 83.8 %block.1 = (bf16[1536,128]{1,0:T(8,128)(2,1)}, bf16[1536,128]{1,0:T(8,128)(2,1)}, bf16[1280,128]{1,0:T(8,128)(2,1)}, bf16[512,128]{1,0:T(8,128)(2,1)}) custom-call(bf16[1536,128]{1,0:T(8,128)(2,1)} %bitcast.9, f32[1,128]{1,0:T(1,128)} %bitcast.12, bf16[3,128,128]{2,1,0:T(8,128)(2,1)} %refs_2_.1, bf16[128,128]{1,0:T(8,128)(2,1)} %refs_3_.1, ...), custom_call_target="tpu_custom_call" | custom-call | tf_op jit(solution)/shard_map/block/pallas_call | solution.py:638
  84.4 2.3 %finish.1 = (bf16[1536,128]{1,0:T(8,128)(2,1)}, bf16[1536,128]{1,0:T(8,128)(2,1)}, f32[1,128]{1,0:T(1,128)}, f32[384,128]{1,0:T(8,128)}, f32[128,128]{1,0:T(8,128)}, /*index=5*/f32[1152,128]{1,0:T(8,128)}) custom-call(bf16[1536,128]{1,0:T(8,128)(2,1)} %get-tuple-element.16.out_s, bf16[1536,128]{1,0:T(8,128)(2,1)} %get-tuple-element.17.gf_s, ...), custom_call_target="tpu_custom_call" | custom-call | tf_op jit(solution)/shard_map/finish/pallas_call | solution.py:708

commit v6 on v4

--- a/solution.py
+++ b/solution.py
@@ -31,7 +31,7 @@
 EP = 160
 LP = 64
 EB = EP // 16
-ACT_PIECES = ((0, 1), (2,), ())
+ACT_PIECES = ((0,), (1, 2), ())
 OG_PIECES = ((), (0, 1, 2), ())
 
 

time: 86.5 us -> 86.5 us (level)
  no operation moved by 1% of the time
where the time goes in v6:
time: 86.5 us; the launch traced here: 86.3 us
  Pallas kernels  85.7 us (99%)
    pallas_call x1, Pallas kernels, on_device(): pl.pallas_call(lambda *refs: kernel(factor, *refs), out_shape=(sds(full,...  83.4 us
    pallas_call x1, Pallas kernels, on_device(): pl.pallas_call(finish, out_shape=sizes, in_specs=[hbm] * 4, out_specs=(hb...  2.25 us

profile of v6, /device:TPU:1, one launch (start us, length us, event | category | flops | bytes accessed | tf_op | source)
XLA Modules:
  0.0 86.3 jit_solution(7038254528283329731)
XLA Ops:
  0.6 83.4 %block.1 = (bf16[1536,128]{1,0:T(8,128)(2,1)}, bf16[1536,128]{1,0:T(8,128)(2,1)}, bf16[1280,128]{1,0:T(8,128)(2,1)}, bf16[512,128]{1,0:T(8,128)(2,1)}) custom-call(bf16[1536,128]{1,0:T(8,128)(2,1)} %bitcast.9, f32[1,128]{1,0:T(1,128)} %bitcast.12, bf16[3,128,128]{2,1,0:T(8,128)(2,1)} %refs_2_.1, bf16[128,128]{1,0:T(8,128)(2,1)} %refs_3_.1, ...), custom_call_target="tpu_custom_call" | custom-call | tf_op jit(solution)/shard_map/block/pallas_call | solution.py:638
  84.1 2.3 %finish.1 = (bf16[1536,128]{1,0:T(8,128)(2,1)}, bf16[1536,128]{1,0:T(8,128)(2,1)}, f32[1,128]{1,0:T(1,128)}, f32[384,128]{1,0:T(8,128)}, f32[128,128]{1,0:T(8,128)}, /*index=5*/f32[1152,128]{1,0:T(8,128)}) custom-call(bf16[1536,128]{1,0:T(8,128)(2,1)} %get-tuple-element.16.out_s, bf16[1536,128]{1,0:T(8,128)(2,1)} %get-tuple-element.17.gf_s, ...), custom_call_target="tpu_custom_call" | custom-call | tf_op jit(solution)/shard_map/finish/pallas_call | solution.py:708
